TPU v7x, 128 devices: a whole 4x4x4 slice. The times are simulated.
128 devices in a mesh: tile: 16 (over x, y), chan: 8 (over z, core).
Axes of the slice: x: 4, y: 4, z: 4, core: 2. Of those that a mesh axis runs over, the one named last changes fastest.
Arguments:
- fields: bfloat16 [12, 128, 128, 256], P(None, 'tile', 'chan'), may hold values from -6 to 6
- neighbour: int32 [12, 4], replicated, may hold values from 0 to 11
- rotation: int32 [12, 4], replicated, may hold values from 0 to 3
- conv_weight: float32 [7, 7, 256], replicated, may hold values from -0.875 to 0.875
- conv_bias: float32 [256], replicated, may hold values from -3 to 3
- norm_gain: float32 [256], replicated, may hold values from 0.25 to 1.75
- norm_shift: float32 [256], replicated, may hold values from -3 to 3
- weight_in: bfloat16 [256, 1024], replicated, may hold values from -0.375 to 0.375
- bias_in: float32 [1024], replicated, may hold values from -3 to 3
- weight_out: bfloat16 [1024, 256], replicated, may hold values from -0.1875 to 0.1875
- bias_out: float32 [256], replicated, may hold values from -3 to 3
- layer_scale: float32 [256], replicated, may hold values from 0.3 to 1.5
Outputs:
- updated: bfloat16 [12, 128, 128, 256], P(None, 'tile', 'chan')
All inputs are finite; a program needn't handle non-finite values.
Results may differ from a plain program's by a relative error of at most 0.005.
Values may be sent and summed in bfloat16 or wider, within the bound.
A program may use at most 128 MiB of HBM per device.

v0:
```python
import functools

import jax
import jax.numpy as jnp
from jax import lax
from jax.experimental import pallas as pl
from jax.experimental.pallas import tpu as pltpu
from jax.sharding import PartitionSpec as P

F32, BF16 = jnp.float32, jnp.bfloat16
FACES, ROWS, COLS, CH, HID = 12, 8, 16, 256, 1024
LANES = 128
TILES, CHANS = 16, 8
STRIDE = 32
FIRST = 8
PADROWS = ROWS + 6
SIDES = 4
STRIP = FACES * 8
FACES_AT_ONCE = 4


def relay_of(block, depth):
    n = block * 3 + depth
    return {"tile": 2 + n // 4, "chan": 2 + n % 4}


def each_pair(body):
    lax.fori_loop(0, FACES // 2, lambda pair, c: (body(pair), c)[1], 0)


def each_face(body):
    lax.fori_loop(0, FACES, lambda face, c: (body(face), c)[1], 0)


def lanes(half):
    return pl.ds(half * LANES, LANES)


def pair_rows(pair):
    return pl.ds(pl.multiple_of(pair * 16, 16), 16)


def kernel(
    fields, neighbour, rotation, conv_weight, conv_bias, norm_gain, norm_shift,
    weight_in, bias_in, weight_out, bias_out, layer_scale,
    out,
    x, nbr, rot, cw, cb, gain, shift, w_in, b_in, w_out, b_out, scale,
    taps, padded, acc, result,
    send_left, send_right, send_edge, left, right, top, bottom, seam,
    corner_out_left, corner_out_right, corner_left, corner_right, above, below,
    relay_in, relay_all, relay_out,
    local_sems, send_sems, recv_sems, out_sem,
):
    i, j = lax.axis_index("tile"), lax.axis_index("chan")
    has_up, has_down = i > 0, i < TILES - 1
    has_left, has_right = j > 0, j < CHANS - 1
    is_top, is_bottom = i == 0, i == TILES - 1
    is_left, is_right = j == 0, j == CHANS - 1
    is_relay = (i >= 2) & (i < 14) & (j >= 2) & (j < 6)
    number = (i - 2) * 4 + (j - 2)
    block, depth = number // 3, number % 3
    turned_block = 15 - block

    locals_ = [
        pltpu.make_async_copy(src, dst, local_sems.at[n])
        for n, (src, dst) in enumerate(
            [
                (fields, x), (neighbour, nbr), (rotation, rot), (conv_weight, cw), (conv_bias, cb),
                (norm_gain, gain), (norm_shift, shift), (weight_in, w_in), (bias_in, b_in),
                (weight_out, w_out), (bias_out, b_out), (layer_scale, scale),
            ]
        )
    ]
    for copy in locals_:
        copy.start()

    barrier = pltpu.get_barrier_semaphore()

    def greet(tile, chan):
        pl.semaphore_signal(
            barrier, inc=1, device_id={"tile": tile, "chan": chan},
            device_id_type=pl.DeviceIdType.MESH,
        )

    def greet_relay(block_, depth_):
        there = relay_of(block_, depth_)
        greet(there["tile"], there["chan"])

    pl.when(has_up)(lambda: greet(i - 1, j))
    pl.when(has_down)(lambda: greet(i + 1, j))
    pl.when(has_left)(lambda: greet(i, j - 1))
    pl.when(has_right)(lambda: greet(i, j + 1))

    @pl.when(is_relay)
    def _():
        greet(0, 7 - block // 2)
        greet(block, 0)
        greet(TILES - 1, block // 2)
        greet(turned_block, CHANS - 1)

    @pl.when(is_top)
    def _():
        for half in range(2):
            for k in range(3):
                greet_relay(2 * j + half, k)

    @pl.when(is_bottom)
    def _():
        for half in range(2):
            for k in range(3):
                greet_relay(15 - (2 * j + half), k)

    def greet_side(to_block):
        for k in range(3):
            greet_relay(to_block(i), k)

        @pl.when(has_up)
        def _():
            for k in range(3):
                greet_relay(to_block(i - 1), k)

        @pl.when(has_down)
        def _():
            for k in range(3):
                greet_relay(to_block(i + 1), k)

    pl.when(is_left)(lambda: greet_side(lambda row: 15 - row))
    pl.when(is_right)(lambda: greet_side(lambda row: row))

    def as_int(flag):
        return flag.astype(jnp.int32)

    expected = (
        as_int(has_up) + as_int(has_down) + as_int(has_left) + as_int(has_right)
        + 6 * as_int(is_top) + 6 * as_int(is_bottom) + 3 * as_int(is_left) + 3 * as_int(is_right)
        + as_int(is_relay) * (4 + 2 * (as_int(block > 0) + as_int(block < 15)))
    )

    locals_[0].wait()

    def unpack(face):
        for half in range(2):
            for r in range(ROWS):
                padded[face, half, pl.ds((r + 3) * STRIDE + FIRST, COLS), :] = x[
                    face, r, :, lanes(half)
                ].astype(F32)
        zero = jnp.zeros((8, LANES), F32)
        for half in range(2):
            for r in (0, 1, 2, 11, 12, 13):
                padded[face, half, pl.ds(r * STRIDE, 8), :] = zero
                padded[face, half, pl.ds(r * STRIDE + FIRST + COLS, 8), :] = zero

    each_face(unpack)

    def column(face, half, first_row, c):
        return padded[face, half, pl.ds(first_row * STRIDE + c + FIRST, 8, stride=STRIDE), :]

    def pack_columns(pair):
        for half in range(2):
            for k in range(3):
                for target, c in ((send_left, k), (send_right, COLS - 1 - k)):
                    target[k, pair_rows(pair), lanes(half)] = jnp.concatenate(
                        [column(2 * pair + e, half, 3, c) for e in range(2)], axis=0
                    ).astype(BF16)

    each_pair(pack_columns)

    def pack_edge(row_of):
        def body(pair):
            for half in range(2):
                for seg in range(2):
                    for k in range(3):
                        at = pl.ds((row_of(k) + 3) * STRIDE + FIRST + 8 * seg, 8)
                        send_edge[seg, k, pair_rows(pair), lanes(half)] = jnp.concatenate(
                            [padded[2 * pair + e, half, at, :] for e in range(2)], axis=0
                        ).astype(BF16)

        each_pair(body)

    pl.when(is_top)(lambda: pack_edge(lambda k: k))
    pl.when(is_bottom)(lambda: pack_edge(lambda k: ROWS - 1 - k))

    pl.semaphore_wait(barrier, expected)

    def remote(src, dst, send, recv, where):
        return pltpu.make_async_remote_copy(
            src_ref=src, dst_ref=dst, send_sem=send_sems.at[send], recv_sem=recv_sems.at[recv],
            device_id=where, device_id_type=pl.DeviceIdType.MESH,
        )

    LEFT, RIGHT, TOP, BOTTOM, SEAM, CORNER_L, CORNER_R, ABOVE, BELOW, RELAY = range(10)

    edge_sends = [
        (is_top, [
            remote(send_edge.at[seg, k], relay_in.at[0], 3 * seg + k, RELAY,
                   relay_of(15 - (2 * j + seg), k))
            for seg in range(2) for k in range(3)
        ]),
        (is_bottom, [
            remote(send_edge.at[seg, k], relay_in.at[2], 3 * seg + k, RELAY,
                   relay_of(2 * j + seg, k))
            for seg in range(2) for k in range(3)
        ]),
        (is_left, [
            remote(send_left.at[k], relay_in.at[1], 6 + k, RELAY, relay_of(i, k))
            for k in range(3)
        ]),
        (is_right, [
            remote(send_right.at[k], relay_in.at[3], 6 + k, RELAY, relay_of(15 - i, k))
            for k in range(3)
        ]),
    ]
    halo_sends = [
        (has_up, [remote(x.at[:, pl.ds(0, 3)], bottom, 9, BOTTOM, {"tile": i - 1, "chan": j})]),
        (has_down, [remote(x.at[:, pl.ds(ROWS - 3, 3)], top, 10, TOP, {"tile": i + 1, "chan": j})]),
        (has_left, [remote(send_left, right, 11, RIGHT, {"tile": i, "chan": j - 1})]),
        (has_right, [remote(send_right, left, 12, LEFT, {"tile": i, "chan": j + 1})]),
    ]
    corner_sends = [
        (has_left, [remote(corner_out_left, corner_right, 13, CORNER_R, {"tile": i, "chan": j - 1})]),
        (has_right, [remote(corner_out_right, corner_left, 14, CORNER_L, {"tile": i, "chan": j + 1})]),
    ]
    relay_sends = [
        (is_relay, [
            remote(relay_out.at[0], seam.at[block % 2, depth], 15, SEAM,
                   {"tile": 0, "chan": block // 2}),
            remote(relay_out.at[2], seam.at[turned_block % 2, depth], 16, SEAM,
                   {"tile": TILES - 1, "chan": turned_block // 2}),
            remote(relay_out.at[1], left.at[depth], 17, LEFT, {"tile": turned_block, "chan": 0}),
            remote(relay_out.at[3], right.at[depth], 18, RIGHT, {"tile": block, "chan": CHANS - 1}),
        ]),
        (is_relay & (turned_block < 15), [
            remote(relay_out.at[1], above.at[depth], 19, ABOVE, {"tile": turned_block + 1, "chan": 0}),
        ]),
        (is_relay & (turned_block > 0), [
            remote(relay_out.at[1], below.at[depth], 20, BELOW, {"tile": turned_block - 1, "chan": 0}),
        ]),
        (is_relay & (block < 15), [
            remote(relay_out.at[3], above.at[depth], 21, ABOVE, {"tile": block + 1, "chan": CHANS - 1}),
        ]),
        (is_relay & (block > 0), [
            remote(relay_out.at[3], below.at[depth], 22, BELOW, {"tile": block - 1, "chan": CHANS - 1}),
        ]),
    ]

    def start_all(sends):
        for condition, copies in sends:
            @pl.when(condition)
            def _():
                for copy in copies:
                    copy.start()

    def arrived(buffer, recv):
        pltpu.make_async_copy(buffer, buffer, recv_sems.at[recv]).wait()

    start_all(edge_sends)
    start_all(halo_sends)

    locals_[1].wait()
    locals_[2].wait()

    @pl.when(is_relay)
    def _():
        arrived(relay_in, RELAY)
        row = lax.broadcasted_iota(jnp.int32, (STRIP, STRIP), 0)
        col = lax.broadcasted_iota(jnp.int32, (STRIP, STRIP), 1)
        turn = (row // 8 * 8 + 7 - row % 8 == col).astype(BF16)
        for side in range(SIDES):
            strip = relay_in[side]
            relay_all[0, pl.ds(side * FACES, FACES)] = strip.astype(F32).reshape(FACES, 8, CH)
            relay_all[1, pl.ds(side * FACES, FACES)] = jnp.dot(
                turn, strip, preferred_element_type=F32
            ).reshape(FACES, 8, CH)

        def choose(pair):
            for side in range(SIDES):
                chosen = []
                for e in range(2):
                    source = (side + 6 - rot[2 * pair + e, side]) & 3
                    same = ((source + 1) & 3) >> 1
                    flip = same if side in (1, 2) else 1 - same
                    chosen.append(relay_all[flip, source * FACES + nbr[2 * pair + e, side]])
                relay_out[side, pair_rows(pair), :] = jnp.concatenate(chosen, axis=0).astype(BF16)

        each_pair(choose)

    start_all(relay_sends)

    locals_[3].wait()
    locals_[4].wait()
    for half in range(2):
        for a in range(7):
            for b in range(7):
                taps[half, a * 7 + b] = jnp.broadcast_to(cw[a, pl.ds(b, 1), lanes(half)], (8, LANES))

    def convolve(face, half, group, total, rows, shifts):
        for b in shifts:
            cells = {
                r: padded[face, half, pl.ds(r * STRIDE + FIRST - 3 + b + 8 * group, 8), :]
                for r in rows
            }
            for a in range(7):
                tap = taps[half, a * 7 + b]
                for r in range(ROWS):
                    if r + a in cells and r in total:
                        total[r] = total[r] + tap * cells[r + a]
        return total

    own = range(3, 11)
    groups = [(half, group) for half in range(2) for group in range(2)]

    def total_of(face, half, group, rows):
        return {r: acc[face, r, pl.ds(8 * group, 8), lanes(half)] for r in rows}

    def keep(face, half, group, total):
        for r, value in total.items():
            acc[face, r, pl.ds(8 * group, 8), lanes(half)] = value

    def inner(face):
        for half, group in groups:
            bias = jnp.broadcast_to(cb[:, lanes(half)], (8, LANES))
            total = {r: bias for r in range(ROWS)}
            shifts = range(3, 7) if group == 0 else range(4)
            keep(face, half, group, convolve(face, half, group, total, own, shifts))

    each_face(inner)

    def unpack_rows(buffer, first_row):
        def body(face):
            for half in range(2):
                for r in range(3):
                    padded[face, half, pl.ds((first_row + r) * STRIDE + FIRST, COLS), :] = buffer[
                        face, r, :, lanes(half)
                    ].astype(F32)

        each_face(body)

    def unpack_seam(row_of):
        def body(pair):
            for half in range(2):
                for seg in range(2):
                    for k in range(3):
                        both = seam[seg, k, pair_rows(pair), lanes(half)].astype(F32)
                        for e in range(2):
                            padded[
                                2 * pair + e, half, pl.ds(row_of(k) * STRIDE + FIRST + 8 * seg, 8), :
                            ] = both[8 * e : 8 * e + 8]

        each_pair(body)

    @pl.when(has_up)
    def _():
        arrived(top, TOP)
        unpack_rows(top, 0)

    @pl.when(has_down)
    def _():
        arrived(bottom, BOTTOM)
        unpack_rows(bottom, 11)

    @pl.when(is_top)
    def _():
        arrived(seam, SEAM)
        unpack_seam(lambda k: 2 - k)

    @pl.when(is_bottom)
    def _():
        arrived(seam, SEAM)
        unpack_seam(lambda k: 11 + k)

    sublane = lax.broadcasted_iota(jnp.int32, (8, LANES), 0)

    def pack_corners(pair):
        for half in range(2):
            for k in range(3):
                for target, c in ((corner_out_left, k), (corner_out_right, COLS - 1 - k)):
                    target[k, pair_rows(pair), lanes(half)] = jnp.concatenate(
                        [
                            jnp.where(
                                sublane < 4,
                                column(2 * pair + e, half, 0, c),
                                column(2 * pair + e, half, 6, c),
                            )
                            for e in range(2)
                        ],
                        axis=0,
                    ).astype(BF16)

    each_pair(pack_corners)
    start_all(corner_sends)

    def unpack_columns(buffer, col_of):
        def body(pair):
            for half in range(2):
                for k in range(3):
                    both = buffer[k, pair_rows(pair), lanes(half)].astype(F32)
                    for e in range(2):
                        padded[
                            2 * pair + e, half,
                            pl.ds(3 * STRIDE + FIRST + col_of(k), 8, stride=STRIDE), :
                        ] = both[8 * e : 8 * e + 8]

        each_pair(body)

    def unpack_corner(buffer, col_of, parts):
        def body(pair):
            for half in range(2):
                for k in range(3):
                    both = buffer[k, pair_rows(pair), lanes(half)].astype(F32)
                    for e in range(2):
                        for sub, row in parts:
                            padded[
                                2 * pair + e, half,
                                pl.ds(row * STRIDE + FIRST + col_of(k), 3, stride=STRIDE), :
                            ] = both[8 * e + sub : 8 * e + sub + 3]

        each_pair(body)

    def at_left(k):
        return -1 - k

    def at_right(k):
        return COLS + k

    arrived(left, LEFT)
    unpack_columns(left, at_left)
    arrived(right, RIGHT)
    unpack_columns(right, at_right)

    def sides(face):
        for half, group in groups:
            total = total_of(face, half, group, range(ROWS))
            shifts = range(3) if group == 0 else range(4, 7)
            keep(face, half, group, convolve(face, half, group, total, own, shifts))

    each_face(sides)

    @pl.when(has_left)
    def _():
        arrived(corner_left, CORNER_L)
        unpack_corner(corner_left, at_left, ((0, 0), (5, 11)))

    @pl.when(has_right)
    def _():
        arrived(corner_right, CORNER_R)
        unpack_corner(corner_right, at_right, ((0, 0), (5, 11)))

    for at_edge, col_of in ((is_left, at_left), (is_right, at_right)):
        @pl.when(at_edge & has_up)
        def _():
            arrived(above, ABOVE)
            unpack_corner(above, col_of, ((5, 0),))

        @pl.when(at_edge & has_down)
        def _():
            arrived(below, BELOW)
            unpack_corner(below, col_of, ((0, 11),))

    def ends(face):
        for half, group in groups:
            for rows, halo in ((range(3), range(3)), (range(5, 8), range(11, 14))):
                total = total_of(face, half, group, rows)
                keep(face, half, group, convolve(face, half, group, total, halo, range(7)))

    each_face(ends)

    for copy in locals_[5:]:
        copy.wait()

    def finished(first):
        return pltpu.make_async_copy(
            result.at[pl.ds(first, FACES_AT_ONCE)], out.at[pl.ds(first, FACES_AT_ONCE)], out_sem
        )

    def pointwise(step, carry):
        first = step * FACES_AT_ONCE
        faces = pl.ds(first, FACES_AT_ONCE)
        cells = FACES_AT_ONCE * ROWS * COLS
        values = acc[faces].reshape(cells, CH).astype(BF16).astype(F32)
        mean = jnp.mean(values, axis=-1, keepdims=True)
        apart = values - mean
        spread = jnp.mean(apart * apart, axis=-1, keepdims=True)
        normed = (apart * lax.rsqrt(spread + 1e-6) * gain[...] + shift[...]).astype(BF16)
        hidden = jnp.dot(normed, w_in[...], preferred_element_type=F32) + b_in[...]
        inner_ = hidden * (0.7978845608028654 + 0.035677408136300125 * (hidden * hidden))
        hidden = (hidden * (1.0 + jnp.tanh(inner_))).astype(BF16)
        update = 0.5 * jnp.dot(hidden, w_out[...], preferred_element_type=F32) + b_out[...]
        residual = x[faces].reshape(cells, CH).astype(F32)
        result[faces] = (residual + scale[...] * update).astype(BF16).reshape(
            FACES_AT_ONCE, ROWS, COLS, CH
        )
        finished(first).start()
        return carry

    lax.fori_loop(0, FACES // FACES_AT_ONCE, pointwise, 0)
    pltpu.make_async_copy(result, out, out_sem).wait()

    for condition, copies in edge_sends + halo_sends + corner_sends + relay_sends:
        @pl.when(condition)
        def _():
            for copy in copies:
                copy.wait_send()


def block(fields, neighbour, rotation, conv_weight, conv_bias, norm_gain, norm_shift,
          weight_in, bias_in, weight_out, bias_out, layer_scale):
    def row(vector):
        return vector.reshape(1, -1)

    anywhere = pl.BlockSpec(memory_space=pl.ANY)
    strip = pltpu.VMEM((3, STRIP, CH), BF16)
    halo_rows = pltpu.VMEM((FACES, 3, COLS, CH), BF16)
    return pl.pallas_call(
        kernel,
        out_shape=jax.ShapeDtypeStruct(fields.shape, BF16),
        in_specs=[anywhere] * 12,
        out_specs=anywhere,
        scratch_shapes=[
            pltpu.VMEM(fields.shape, BF16),
            pltpu.SMEM((FACES, SIDES), jnp.int32),
            pltpu.SMEM((FACES, SIDES), jnp.int32),
            pltpu.VMEM((7, 7, CH), F32),
            pltpu.VMEM((1, CH), F32),
            pltpu.VMEM((1, CH), F32),
            pltpu.VMEM((1, CH), F32),
            pltpu.VMEM((CH, HID), BF16),
            pltpu.VMEM((1, HID), F32),
            pltpu.VMEM((HID, CH), BF16),
            pltpu.VMEM((1, CH), F32),
            pltpu.VMEM((1, CH), F32),
            pltpu.VMEM((2, 49, 8, LANES), F32),
            pltpu.VMEM((FACES, 2, PADROWS * STRIDE, LANES), F32),
            pltpu.VMEM(fields.shape, F32),
            pltpu.VMEM(fields.shape, BF16),
            strip, strip,
            pltpu.VMEM((2, 3, STRIP, CH), BF16),
            strip, strip,
            halo_rows, halo_rows,
            pltpu.VMEM((2, 3, STRIP, CH), BF16),
            strip, strip, strip, strip, strip, strip,
            pltpu.VMEM((SIDES, STRIP, CH), BF16),
            pltpu.VMEM((2, SIDES * FACES, 8, CH), F32),
            pltpu.VMEM((SIDES, STRIP, CH), BF16),
            pltpu.SemaphoreType.DMA((12,)),
            pltpu.SemaphoreType.DMA((23,)),
            pltpu.SemaphoreType.DMA((10,)),
            pltpu.SemaphoreType.DMA,
        ],
        compiler_params=pltpu.CompilerParams(
            collective_id=0, has_side_effects=True, vmem_limit_bytes=48 * 2**20
        ),
        name="convnext_block",
    )(
        fields, neighbour, rotation, conv_weight, row(conv_bias), row(norm_gain), row(norm_shift),
        weight_in, row(bias_in), weight_out, row(bias_out), row(layer_scale),
    )


def solution(mesh):
    cells = P(None, "tile", "chan", None)
    return jax.shard_map(
        block, mesh=mesh, in_specs=(cells,) + (P(),) * 11, out_specs=cells, check_vma=False
    )
```

profile of v0, /device:TPU:0, one launch (start us, length us, event | category | flops | bytes accessed | tf_op | source)
XLA Modules:
  0.0 43.1 jit_solution(937993165142426267)
XLA Ops:
  0.0 0.0 copy-start.10
  0.0 0.7 %copy-done.10 = s32[12,4]{0,1:T(4,128)S(1)} copy-done((s32[12,4]{0,1:T(4,128)S(1)}, s32[12,4]{0,1:T(4,128)}, u32[]{:S(2)}) %copy-start.10) | copy-done | bytes 216
  0.7 0.0 copy-start.11
  0.7 0.1 copy.13.neighbour
  0.8 0.6 %copy-done.11 = s32[12,4]{0,1:T(4,128)S(1)} copy-done((s32[12,4]{0,1:T(4,128)S(1)}, s32[12,4]{0,1:T(4,128)}, u32[]{:S(2)}) %copy-start.11) | copy-done | bytes 216
  1.4 0.0 copy-start.4
  1.4 0.0 copy-start.5
  1.4 0.0 copy-start.6
  1.4 0.0 copy-start.7
  1.4 0.0 copy-start.8
  1.4 0.0 copy-start.9
  1.4 0.1 copy.14.rotation
  1.5 0.6 %copy-done.4 = f32[1024]{0:T(1024)S(1)} copy-done((f32[1024]{0:T(1024)S(1)}, f32[1024]{0:T(1024)}, u32[]{:S(2)}) %copy-start.4) | copy-done | bytes 4120
  2.1 0.0 copy-done.5
  2.1 0.0 copy-done.6
  2.1 0.0 copy-done.7
  2.1 0.0 copy-done.8
  2.1 0.0 copy-done.9
  2.1 0.0 copy-start
  2.1 1.1 %copy-done = bf16[12,8,16,256]{3,2,1,0:T(8,128)(2,1)S(1)} copy-done((bf16[12,8,16,256]{3,2,1,0:T(8,128)(2,1)S(1)}, bf16[12,8,16,256]{3,2,1,0:T(8,128)(2,1)}, u32[]{:S(2)}) %copy-start) | copy-done | bytes 786456
  3.3 0.0 copy-start.1
  3.3 1.0 %copy-done.1 = bf16[256,1024]{1,0:T(8,128)(2,1)S(1)} copy-done((bf16[256,1024]{1,0:T(8,128)(2,1)S(1)}, bf16[256,1024]{1,0:T(8,128)(2,1)}, u32[]{:S(2)}) %copy-start.1) | copy-done | bytes 524312
  4.3 0.0 copy-start.2
  4.3 1.0 %copy-done.2 = bf16[1024,256]{1,0:T(8,128)(2,1)S(1)} copy-done((bf16[1024,256]{1,0:T(8,128)(2,1)S(1)}, bf16[1024,256]{1,0:T(8,128)(2,1)}, u32[]{:S(2)}) %copy-start.2) | copy-done | bytes 524312
  5.3 0.0 copy-start.3
  5.3 0.8 %copy-done.3 = f32[7,7,256]{2,1,0:T(8,128)S(1)} copy-done((f32[7,7,256]{2,1,0:T(8,128)S(1)}, f32[7,7,256]{2,1,0:T(8,128)}, u32[]{:S(2)}) %copy-start.3) | copy-done | bytes 50200
  6.2 36.0 %convnext_block.1 = bf16[12,8,16,256]{3,2,1,0:T(8,128)(2,1)S(1)} custom-call(bf16[12,8,16,256]{3,2,1,0:T(8,128)(2,1)S(1)} %copy-done, s32[12,4]{1,0:T(8,128)S(1)} %copy.13.neighbour, s32[12,4]{1,0:T(8,128)S(1)} %copy.14.rotation, f32[7,7,256]{2,1,0:T(8,128)S(1)} %copy-done.3, f32[1,256]{1,0:T(1,128)S(1)} %bitcast.7, f32[1,256]{1,0:T(1,128)S(1)} %bitcast.8, ...), custom_call_target="tpu_custom_call" | custom-call | tf_op jit(solution)/shard_map/convnext_block/pallas_call | solution.py:513
  42.2 0.9 %copy.16 = bf16[12,8,16,256]{3,2,1,0:T(8,128)(2,1)} copy(bf16[12,8,16,256]{3,2,1,0:T(8,128)(2,1)S(1)} %convnext_block.1) | data formatting | bytes 1572864
Async XLA Ops:
  0.0 0.7 %copy-start.10 = (s32[12,4]{0,1:T(4,128)S(1)}, s32[12,4]{0,1:T(4,128)}, u32[]{:S(2)}) copy-start(s32[12,4]{0,1:T(4,128)} %param.13) | copy-start | bytes 580
  0.7 0.7 %copy-start.11 = (s32[12,4]{0,1:T(4,128)S(1)}, s32[12,4]{0,1:T(4,128)}, u32[]{:S(2)}) copy-start(s32[12,4]{0,1:T(4,128)} %param.14) | copy-start | bytes 580
  1.4 0.7 %copy-start.4 = (f32[1024]{0:T(1024)S(1)}, f32[1024]{0:T(1024)}, u32[]{:S(2)}) copy-start(f32[1024]{0:T(1024)} %param.20) | copy-start | bytes 12292
  1.4 0.7 %copy-start.5 = (f32[256]{0:T(256)S(1)}, f32[256]{0:T(256)}, u32[]{:S(2)}) copy-start(f32[256]{0:T(256)} %param.16) | copy-start | bytes 3076
  1.4 0.7 %copy-start.6 = (f32[256]{0:T(256)S(1)}, f32[256]{0:T(256)}, u32[]{:S(2)}) copy-start(f32[256]{0:T(256)} %param.17) | copy-start | bytes 3076
  1.4 0.7 %copy-start.7 = (f32[256]{0:T(256)S(1)}, f32[256]{0:T(256)}, u32[]{:S(2)}) copy-start(f32[256]{0:T(256)} %param.18) | copy-start | bytes 3076
  1.4 0.7 %copy-start.8 = (f32[256]{0:T(256)S(1)}, f32[256]{0:T(256)}, u32[]{:S(2)}) copy-start(f32[256]{0:T(256)} %param.22) | copy-start | bytes 3076
  1.4 0.7 %copy-start.9 = (f32[256]{0:T(256)S(1)}, f32[256]{0:T(256)}, u32[]{:S(2)}) copy-start(f32[256]{0:T(256)} %param.23) | copy-start | bytes 3076
  2.1 1.1 %copy-start = (bf16[12,8,16,256]{3,2,1,0:T(8,128)(2,1)S(1)}, bf16[12,8,16,256]{3,2,1,0:T(8,128)(2,1)}, u32[]{:S(2)}) copy-start(bf16[12,8,16,256]{3,2,1,0:T(8,128)(2,1)} %fields.1) | copy-start | bytes 2359300
  3.3 1.0 %copy-start.1 = (bf16[256,1024]{1,0:T(8,128)(2,1)S(1)}, bf16[256,1024]{1,0:T(8,128)(2,1)}, u32[]{:S(2)}) copy-start(bf16[256,1024]{1,0:T(8,128)(2,1)} %weight_in.1) | copy-start | bytes 1572868
  4.3 1.0 %copy-start.2 = (bf16[1024,256]{1,0:T(8,128)(2,1)S(1)}, bf16[1024,256]{1,0:T(8,128)(2,1)}, u32[]{:S(2)}) copy-start(bf16[1024,256]{1,0:T(8,128)(2,1)} %weight_out.1) | copy-start | bytes 1572868
  5.3 0.8 %copy-start.3 = (f32[7,7,256]{2,1,0:T(8,128)S(1)}, f32[7,7,256]{2,1,0:T(8,128)}, u32[]{:S(2)}) copy-start(f32[7,7,256]{2,1,0:T(8,128)} %conv_weight.1) | copy-start | bytes 150532
where the time goes:
time: 43.4 us; the launch traced here: 43.1 us
  Pallas kernels  36 us (83%)
  local copies, waits for them, and re-layouts  7.01 us (16%)
    pallas_call x1, Pallas kernels, block(): pl.pallas_call(kernel, out_shape=jax.ShapeDtypeStruct(fields.shape, BF16)...  36 us
    unnamed x27, local copies, waits for them, and re-layouts  7.01 us

commit v1 on v0

v1 whole, which is shorter than its diff:
```python
import functools

import jax
import jax.numpy as jnp
from jax import lax
from jax.experimental import pallas as pl
from jax.experimental.pallas import tpu as pltpu
from jax.sharding import PartitionSpec as P

F32, BF16 = jnp.float32, jnp.bfloat16
FACES, ROWS, COLS, CH, HID = 12, 8, 16, 256, 1024
LANES = 128
TILES, CHANS = 16, 8
STRIDE = 32
FIRST = 8
PADROWS = ROWS + 6
SIDES = 4
STRIP = FACES * 8
FACES_AT_ONCE = 4


def relay_chan(z):
    return z + 1 + 2 * (z // 2)


def relay_of(block, half):
    x, y = block // 4, block % 4
    if half == 0:
        across, along, z = 3 - y, (5 - x) % 4, (y + 1) % 4
    else:
        across, along, z = y, (x + 2) % 4, (6 - y) % 4
    return {"tile": 4 * across + along, "chan": relay_chan(z)}


def relay_role(i, j):
    across, along = i // 4, i % 4
    first = j == relay_chan((4 - across) % 4)
    second = j == relay_chan((6 - across) % 4)
    block = jnp.where(
        second, 4 * ((along + 2) % 4) + across, 4 * ((5 - along) % 4) + 3 - across
    )
    return first | second, block, second.astype(jnp.int32)


def each_quad(body):
    lax.fori_loop(0, FACES // 4, lambda quad, c: (body(quad), c)[1], 0)


def each_pair(body):
    lax.fori_loop(0, FACES // 2, lambda pair, c: (body(pair), c)[1], 0)


def each_face(body):
    lax.fori_loop(0, FACES, lambda face, c: (body(face), c)[1], 0)


def lanes(half):
    return pl.ds(half * LANES, LANES)


def pair_rows(pair):
    return pl.ds(pl.multiple_of(pair * 16, 16), 16)


def kernel(
    fields, neighbour, rotation, conv_weight, conv_bias, norm_gain, norm_shift,
    weight_in, bias_in, weight_out, bias_out, layer_scale,
    out,
    x, nbr, rot, cw, cb, gain, shift, w_in, b_in, w_out, b_out, scale,
    taps, padded, acc, result,
    send_left, send_right, send_edge, send_corner, left, right, top, bottom, seam, corner,
    relay_in, relay_all, relay_out, relay_first, relay_last,
    local_sems, send_sems, recv_sems, out_sem,
):
    i, j = lax.axis_index("tile"), lax.axis_index("chan")
    has_up, has_down = i > 0, i < TILES - 1
    has_left, has_right = j > 0, j < CHANS - 1
    is_top, is_bottom = i == 0, i == TILES - 1
    is_left, is_right = j == 0, j == CHANS - 1
    is_relay, block, my_half = relay_role(i, j)
    turned_block = 15 - block
    odd = block % 2 == 1

    locals_ = [
        pltpu.make_async_copy(src, dst, local_sems.at[n])
        for n, (src, dst) in enumerate(
            [
                (fields, x), (neighbour, nbr), (rotation, rot), (conv_weight, cw), (conv_bias, cb),
                (norm_gain, gain), (norm_shift, shift), (weight_in, w_in), (bias_in, b_in),
                (weight_out, w_out), (bias_out, b_out), (layer_scale, scale),
            ]
        )
    ]
    for copy in locals_:
        copy.start()

    barrier = pltpu.get_barrier_semaphore()

    def greet(tile, chan):
        pl.semaphore_signal(
            barrier, inc=1, device_id={"tile": tile, "chan": chan},
            device_id_type=pl.DeviceIdType.MESH,
        )

    def greet_relays(block_):
        for half in range(2):
            there = relay_of(block_, half)
            greet(there["tile"], there["chan"])

    pl.when(has_up)(lambda: greet(i - 1, j))
    pl.when(has_down)(lambda: greet(i + 1, j))
    pl.when(has_left)(lambda: greet(i, j - 1))
    pl.when(has_right)(lambda: greet(i, j + 1))
    pl.when(has_up & has_left)(lambda: greet(i - 1, j - 1))
    pl.when(has_up & has_right)(lambda: greet(i - 1, j + 1))
    pl.when(has_down & has_left)(lambda: greet(i + 1, j - 1))
    pl.when(has_down & has_right)(lambda: greet(i + 1, j + 1))

    @pl.when(is_relay)
    def _():
        greet(0, 7 - block // 2)
        greet(block, 0)
        greet(TILES - 1, block // 2)
        greet(turned_block, CHANS - 1)

    def greet_end(to_block):
        greet_relays(to_block(2 * j))
        greet_relays(to_block(2 * j + 1))
        pl.when(has_left)(lambda: greet_relays(to_block(2 * j - 1)))
        pl.when(has_right)(lambda: greet_relays(to_block(2 * j + 2)))

    def greet_side(to_block):
        greet_relays(to_block(i))
        pl.when(has_up)(lambda: greet_relays(to_block(i - 1)))
        pl.when(has_down)(lambda: greet_relays(to_block(i + 1)))

    pl.when(is_top)(lambda: greet_end(lambda t: t))
    pl.when(is_bottom)(lambda: greet_end(lambda t: 15 - t))
    pl.when(is_left)(lambda: greet_side(lambda t: 15 - t))
    pl.when(is_right)(lambda: greet_side(lambda t: t))

    def as_int(flag):
        return flag.astype(jnp.int32)

    not_first, not_last = as_int(block > 0), as_int(block < 15)
    expected = (
        (1 + as_int(has_up) + as_int(has_down)) * (1 + as_int(has_left) + as_int(has_right)) - 1
        + 4 * as_int(is_top) + 4 * as_int(is_bottom) + 2 * as_int(is_left) + 2 * as_int(is_right)
        + as_int(is_relay)
        * (4 + 2 * (not_first + not_last) + 2 * jnp.where(odd, not_last, not_first))
    )

    locals_[0].wait()

    def unpack(face):
        for half in range(2):
            for r in range(ROWS):
                padded[face, half, pl.ds((r + 3) * STRIDE + FIRST, COLS), :] = x[
                    face, r, :, lanes(half)
                ].astype(F32)
        zero = jnp.zeros((8, LANES), F32)
        for half in range(2):
            for r in (0, 1, 2, 11, 12, 13):
                padded[face, half, pl.ds(r * STRIDE, 8), :] = zero
                padded[face, half, pl.ds(r * STRIDE + FIRST + COLS, 8), :] = zero

    each_face(unpack)

    def column(face, half, first_row, c):
        return padded[face, half, pl.ds(first_row * STRIDE + c + FIRST, 8, stride=STRIDE), :]

    sublane = lax.broadcasted_iota(jnp.int32, (8, LANES), 0)

    def lower_half(a, b):
        return jnp.where(sublane < 4, a, pltpu.roll(b, 4, 0))

    def upper_half(a, b):
        return jnp.where(sublane < 4, pltpu.roll(a, 4, 0), b)

    def two(a, b):
        return jnp.concatenate([a, b], axis=0).astype(BF16)

    def pack_columns(quad):
        for half in range(2):
            for k in range(3):
                for side, (target, c) in enumerate(((send_left, k), (send_right, COLS - 1 - k))):
                    cells = [column(4 * quad + e, half, 3, c) for e in range(4)]
                    for e in range(2):
                        target[half, k, pair_rows(2 * quad + e), :] = two(*cells[2 * e : 2 * e + 2])
                    send_corner[2 * side, half, k, pair_rows(quad), :] = two(
                        lower_half(*cells[:2]), lower_half(*cells[2:])
                    )
                    send_corner[2 * side + 1, half, k, pair_rows(quad), :] = two(
                        upper_half(*cells[:2]), upper_half(*cells[2:])
                    )

    each_quad(pack_columns)

    def pack_edge(row_of):
        def body(pair):
            for half in range(2):
                for seg in range(2):
                    for k in range(3):
                        at = pl.ds((row_of(k) + 3) * STRIDE + FIRST + 8 * seg, 8)
                        send_edge[seg, half, k, pair_rows(pair), :] = two(
                            *[padded[2 * pair + e, half, at, :] for e in range(2)]
                        )

        each_pair(body)

    pl.when(is_top)(lambda: pack_edge(lambda k: k))
    pl.when(is_bottom)(lambda: pack_edge(lambda k: ROWS - 1 - k))

    pl.semaphore_wait(barrier, expected)

    def remote(src, dst, send, recv, where):
        return pltpu.make_async_remote_copy(
            src_ref=src, dst_ref=dst, send_sem=send_sems.at[send], recv_sem=recv_sems.at[recv],
            device_id=where, device_id_type=pl.DeviceIdType.MESH,
        )

    LEFT, RIGHT, TOP, BOTTOM, SEAM, RELAY, CORNER = range(7)

    edge_sends = [
        (is_top, [
            remote(send_edge.at[seg, half], relay_in.at[0], 2 * seg + half, RELAY,
                   relay_of(15 - (2 * j + seg), half))
            for seg in range(2) for half in range(2)
        ]),
        (is_bottom, [
            remote(send_edge.at[seg, half], relay_in.at[2], 2 * seg + half, RELAY,
                   relay_of(2 * j + seg, half))
            for seg in range(2) for half in range(2)
        ]),
        (is_left, [
            remote(send_left.at[half], relay_in.at[1], 4 + half, RELAY, relay_of(i, half))
            for half in range(2)
        ]),
        (is_right, [
            remote(send_right.at[half], relay_in.at[3], 4 + half, RELAY, relay_of(15 - i, half))
            for half in range(2)
        ]),
    ]
    halo_sends = [
        (has_up, [remote(x.at[:, pl.ds(0, 3)], bottom, 6, BOTTOM, {"tile": i - 1, "chan": j})]),
        (has_down, [remote(x.at[:, pl.ds(ROWS - 3, 3)], top, 7, TOP, {"tile": i + 1, "chan": j})]),
        (has_left, [remote(send_left, right, 8, RIGHT, {"tile": i, "chan": j - 1})]),
        (has_right, [remote(send_right, left, 9, LEFT, {"tile": i, "chan": j + 1})]),
    ]
    for side, (there, has_side) in enumerate(((j - 1, has_left), (j + 1, has_right))):
        for end, (tile, has_end) in enumerate(((i - 1, has_up), (i + 1, has_down))):
            mine, theirs = 2 * side + end, 3 - (2 * side + end)
            halo_sends.append((
                has_side & has_end,
                [remote(send_corner.at[mine], corner.at[theirs], 10 + mine, CORNER + theirs,
                        {"tile": tile, "chan": there})],
            ))

    def pass_on(source, corner_at, send, tile, chan):
        return remote(source, corner.at[corner_at, my_half], send, CORNER + corner_at,
                      {"tile": tile, "chan": chan})

    relay_sends = [
        (is_relay, [
            remote(relay_out.at[0], seam.at[block % 2, my_half], 14, SEAM,
                   {"tile": 0, "chan": block // 2}),
            remote(relay_out.at[2], seam.at[turned_block % 2, my_half], 15, SEAM,
                   {"tile": TILES - 1, "chan": turned_block // 2}),
            remote(relay_out.at[1], left.at[my_half], 16, LEFT, {"tile": turned_block, "chan": 0}),
            remote(relay_out.at[3], right.at[my_half], 17, RIGHT,
                   {"tile": block, "chan": CHANS - 1}),
        ]),
        (is_relay & (turned_block < 15),
         [pass_on(relay_last.at[1], 0, 18, turned_block + 1, 0)]),
        (is_relay & (turned_block > 0),
         [pass_on(relay_first.at[1], 1, 19, turned_block - 1, 0)]),
        (is_relay & (block < 15),
         [pass_on(relay_last.at[3], 2, 20, block + 1, CHANS - 1)]),
        (is_relay & (block > 0),
         [pass_on(relay_first.at[3], 3, 21, block - 1, CHANS - 1)]),
        (is_relay & odd & (block < 15), [
            pass_on(relay_last.at[0], 0, 22, 0, block // 2 + 1),
            pass_on(relay_first.at[2], 3, 23, TILES - 1, turned_block // 2 - 1),
        ]),
        (is_relay & ~odd & (block > 0), [
            pass_on(relay_first.at[0], 2, 22, 0, block // 2 - 1),
            pass_on(relay_last.at[2], 1, 23, TILES - 1, turned_block // 2 + 1),
        ]),
    ]

    def start_all(sends):
        for condition, copies in sends:
            @pl.when(condition)
            def _():
                for copy in copies:
                    copy.start()

    def arrived(buffer, recv):
        pltpu.make_async_copy(buffer, buffer, recv_sems.at[recv]).wait()

    start_all(edge_sends)
    start_all(halo_sends)

    locals_[1].wait()
    locals_[2].wait()

    @pl.when(is_relay)
    def _():
        arrived(relay_in, RELAY)
        row = lax.broadcasted_iota(jnp.int32, (STRIP, STRIP), 0)
        col = lax.broadcasted_iota(jnp.int32, (STRIP, STRIP), 1)
        turn = (row // 8 * 8 + 7 - row % 8 == col).astype(BF16)
        for side in range(SIDES):
            for k in range(3):
                strip = relay_in[side, k]
                at = pl.ds(side * FACES, FACES)
                relay_all[0, at, k] = strip.astype(F32).reshape(FACES, 8, LANES)
                relay_all[1, at, k] = jnp.dot(turn, strip, preferred_element_type=F32).reshape(
                    FACES, 8, LANES
                )

        def choose(quad):
            for side in range(SIDES):
                chosen = []
                for e in range(4):
                    source = (side + 6 - rot[side, 4 * quad + e]) & 3
                    same = ((source + 1) & 3) >> 1
                    flip = same if side in (1, 2) else 1 - same
                    chosen.append(relay_all[flip, source * FACES + nbr[side, 4 * quad + e]])
                for k in range(3):
                    cells = [strip[k] for strip in chosen]
                    for e in range(2):
                        relay_out[side, k, pair_rows(2 * quad + e), :] = two(
                            *cells[2 * e : 2 * e + 2]
                        )
                    relay_first[side, k, pair_rows(quad), :] = two(
                        lower_half(*cells[:2]), lower_half(*cells[2:])
                    )
                    relay_last[side, k, pair_rows(quad), :] = two(
                        upper_half(*cells[:2]), upper_half(*cells[2:])
                    )

        each_quad(choose)

    start_all(relay_sends)

    locals_[3].wait()
    locals_[4].wait()
    for half in range(2):
        for a in range(7):
            for b in range(7):
                taps[half, a * 7 + b] = jnp.broadcast_to(cw[a, pl.ds(b, 1), lanes(half)], (8, LANES))

    def convolve(face, half, group, total, rows, shifts):
        for b in shifts:
            cells = {
                r: padded[face, half, pl.ds(r * STRIDE + FIRST - 3 + b + 8 * group, 8), :]
                for r in rows
            }
            for a in range(7):
                tap = taps[half, a * 7 + b]
                for r in range(ROWS):
                    if r + a in cells and r in total:
                        total[r] = total[r] + tap * cells[r + a]
        return total

    own = range(3, 11)
    groups = [(half, group) for half in range(2) for group in range(2)]

    def total_of(face, half, group, rows):
        return {r: acc[face, r, pl.ds(8 * group, 8), lanes(half)] for r in rows}

    def keep(face, half, group, total):
        for r, value in total.items():
            acc[face, r, pl.ds(8 * group, 8), lanes(half)] = value

    def inner(face):
        for half, group in groups:
            bias = jnp.broadcast_to(cb[:, lanes(half)], (8, LANES))
            total = {r: bias for r in range(ROWS)}
            shifts = range(3, 7) if group == 0 else range(4)
            keep(face, half, group, convolve(face, half, group, total, own, shifts))

    each_face(inner)

    def unpack_rows(buffer, first_row):
        def body(face):
            for half in range(2):
                for r in range(3):
                    padded[face, half, pl.ds((first_row + r) * STRIDE + FIRST, COLS), :] = buffer[
                        face, r, :, lanes(half)
                    ].astype(F32)

        each_face(body)

    def unpack_seam(row_of):
        def body(pair):
            for half in range(2):
                for seg in range(2):
                    for k in range(3):
                        both = seam[seg, half, k, pair_rows(pair), :].astype(F32)
                        for e in range(2):
                            padded[
                                2 * pair + e, half, pl.ds(row_of(k) * STRIDE + FIRST + 8 * seg, 8), :
                            ] = both[8 * e : 8 * e + 8]

        each_pair(body)

    @pl.when(has_up)
    def _():
        arrived(top, TOP)
        unpack_rows(top, 0)

    @pl.when(has_down)
    def _():
        arrived(bottom, BOTTOM)
        unpack_rows(bottom, 11)

    @pl.when(is_top)
    def _():
        arrived(seam, SEAM)
        unpack_seam(lambda k: 2 - k)

    @pl.when(is_bottom)
    def _():
        arrived(seam, SEAM)
        unpack_seam(lambda k: 11 + k)

    def unpack_columns(buffer, col_of):
        def body(pair):
            for half in range(2):
                for k in range(3):
                    both = buffer[half, k, pair_rows(pair), :].astype(F32)
                    for e in range(2):
                        padded[
                            2 * pair + e, half,
                            pl.ds(3 * STRIDE + FIRST + col_of(k), 8, stride=STRIDE), :
                        ] = both[8 * e : 8 * e + 8]

        each_pair(body)

    def unpack_corner(at, beside, end):
        first_col = -4 if at < 2 else COLS

        def body(quad):
            for half in range(2):
                for k in range(3):
                    cells = corner[at, half, k, pair_rows(quad), :].astype(F32)
                    for e in range(4):
                        if beside:
                            col = -1 - k if at < 2 else COLS + k
                            first, row = (1, 0) if end == 0 else (0, 11)
                            padded[
                                4 * quad + e, half,
                                pl.ds(row * STRIDE + FIRST + col, 3, stride=STRIDE), :
                            ] = cells[4 * e + first : 4 * e + first + 3]
                        else:
                            row = 2 - k if end == 0 else 11 + k
                            padded[
                                4 * quad + e, half, pl.ds(row * STRIDE + FIRST + first_col, 4), :
                            ] = cells[4 * e : 4 * e + 4]

        each_quad(body)

    def at_left(k):
        return -1 - k

    def at_right(k):
        return COLS + k

    arrived(left, LEFT)
    unpack_columns(left, at_left)
    arrived(right, RIGHT)
    unpack_columns(right, at_right)

    def sides(face):
        for half, group in groups:
            total = total_of(face, half, group, range(ROWS))
            shifts = range(3) if group == 0 else range(4, 7)
            keep(face, half, group, convolve(face, half, group, total, own, shifts))

    each_face(sides)

    for side, (has_side, at_side) in enumerate(((has_left, is_left), (has_right, is_right))):
        for end, (has_end, at_end) in enumerate(((has_up, is_top), (has_down, is_bottom))):
            at = 2 * side + end

            @pl.when(has_side | has_end)
            def _():
                arrived(corner.at[at], CORNER + at)

            pl.when(has_end)(functools.partial(unpack_corner, at, True, end))
            pl.when(at_end & has_side)(functools.partial(unpack_corner, at, False, end))

    def ends(face):
        for half, group in groups:
            for rows, halo in ((range(3), range(3)), (range(5, 8), range(11, 14))):
                total = total_of(face, half, group, rows)
                keep(face, half, group, convolve(face, half, group, total, halo, range(7)))

    each_face(ends)

    for copy in locals_[5:]:
        copy.wait()

    def finished(first):
        return pltpu.make_async_copy(
            result.at[pl.ds(first, FACES_AT_ONCE)], out.at[pl.ds(first, FACES_AT_ONCE)], out_sem
        )

    def pointwise(step, carry):
        first = step * FACES_AT_ONCE
        faces = pl.ds(first, FACES_AT_ONCE)
        cells = FACES_AT_ONCE * ROWS * COLS
        values = acc[faces].reshape(cells, CH).astype(BF16).astype(F32)
        mean = jnp.mean(values, axis=-1, keepdims=True)
        apart = values - mean
        spread = jnp.mean(apart * apart, axis=-1, keepdims=True)
        normed = (apart * lax.rsqrt(spread + 1e-6) * gain[...] + shift[...]).astype(BF16)
        hidden = jnp.dot(normed, w_in[...], preferred_element_type=F32) + b_in[...]
        inner_ = hidden * (0.7978845608028654 + 0.035677408136300125 * (hidden * hidden))
        hidden = (hidden * (1.0 + jnp.tanh(inner_))).astype(BF16)
        update = 0.5 * jnp.dot(hidden, w_out[...], preferred_element_type=F32) + b_out[...]
        residual = x[faces].reshape(cells, CH).astype(F32)
        result[faces] = (residual + scale[...] * update).astype(BF16).reshape(
            FACES_AT_ONCE, ROWS, COLS, CH
        )
        finished(first).start()
        return carry

    lax.fori_loop(0, FACES // FACES_AT_ONCE, pointwise, 0)
    pltpu.make_async_copy(result, out, out_sem).wait()

    for condition, copies in edge_sends + halo_sends + relay_sends:
        @pl.when(condition)
        def _():
            for copy in copies:
                copy.wait_send()


def block(fields, neighbour, rotation, conv_weight, conv_bias, norm_gain, norm_shift,
          weight_in, bias_in, weight_out, bias_out, layer_scale):
    def row(vector):
        return vector.reshape(1, -1)

    anywhere = pl.BlockSpec(memory_space=pl.ANY)
    strip = pltpu.VMEM((2, 3, STRIP, LANES), BF16)
    corners = pltpu.VMEM((4, 2, 3, STRIP // 2, LANES), BF16)
    relayed = pltpu.VMEM((SIDES, 3, STRIP, LANES), BF16)
    relayed_half = pltpu.VMEM((SIDES, 3, STRIP // 2, LANES), BF16)
    halo_rows = pltpu.VMEM((FACES, 3, COLS, CH), BF16)
    return pl.pallas_call(
        kernel,
        out_shape=jax.ShapeDtypeStruct(fields.shape, BF16),
        in_specs=[anywhere] * 12,
        out_specs=anywhere,
        scratch_shapes=[
            pltpu.VMEM(fields.shape, BF16),
            pltpu.SMEM((SIDES, FACES), jnp.int32),
            pltpu.SMEM((SIDES, FACES), jnp.int32),
            pltpu.VMEM((7, 7, CH), F32),
            pltpu.VMEM((1, CH), F32),
            pltpu.VMEM((1, CH), F32),
            pltpu.VMEM((1, CH), F32),
            pltpu.VMEM((CH, HID), BF16),
            pltpu.VMEM((1, HID), F32),
            pltpu.VMEM((HID, CH), BF16),
            pltpu.VMEM((1, CH), F32),
            pltpu.VMEM((1, CH), F32),
            pltpu.VMEM((2, 49, 8, LANES), F32),
            pltpu.VMEM((FACES, 2, PADROWS * STRIDE, LANES), F32),
            pltpu.VMEM(fields.shape, F32),
            pltpu.VMEM(fields.shape, BF16),
            strip, strip,
            pltpu.VMEM((2, 2, 3, STRIP, LANES), BF16),
            corners,
            strip, strip,
            halo_rows, halo_rows,
            pltpu.VMEM((2, 2, 3, STRIP, LANES), BF16),
            corners,
            relayed,
            pltpu.VMEM((2, SIDES * FACES, 3, 8, LANES), F32),
            relayed, relayed_half, relayed_half,
            pltpu.SemaphoreType.DMA((12,)),
            pltpu.SemaphoreType.DMA((24,)),
            pltpu.SemaphoreType.DMA((11,)),
            pltpu.SemaphoreType.DMA,
        ],
        compiler_params=pltpu.CompilerParams(
            collective_id=0, has_side_effects=True, vmem_limit_bytes=63 * 2**20
        ),
        name="convnext_block",
    )(
        fields, neighbour.T, rotation.T, conv_weight, row(conv_bias), row(norm_gain), row(norm_shift),
        weight_in, row(bias_in), weight_out, row(bias_out), row(layer_scale),
    )


def solution(mesh):
    cells = P(None, "tile", "chan", None)
    return jax.shard_map(
        block, mesh=mesh, in_specs=(cells,) + (P(),) * 11, out_specs=cells, check_vma=False
    )
```

time: 43.4 us -> 36.7 us (0.85)
  the two profiles are of different devices: /device:TPU:0 before, /device:TPU:2 now
where the time goes in v1:
time: 36.7 us; the launch traced here: 36.5 us
  Pallas kernels  34.5 us (94%)
  local copies, waits for them, and re-layouts  2.06 us (6%)
    pallas_call x1, Pallas kernels, block(): pl.pallas_call(kernel, out_shape=jax.ShapeDtypeStruct(fields.shape, BF16)...  34.5 us
    unnamed x1, local copies, waits for them, and re-layouts  2.06 us

profile of v1, /device:TPU:2, one launch (start us, length us, event | category | flops | bytes accessed | tf_op | source)
XLA Modules:
  0.0 36.5 jit_solution(15050533154919352674)
XLA Ops:
  0.0 34.5 %convnext_block.1 = bf16[12,8,16,256]{3,2,1,0:T(8,128)(2,1)} custom-call(bf16[12,8,16,256]{3,2,1,0:T(8,128)(2,1)} %fields.1, s32[4,12]{1,0:T(4,128)} %bitcast.9, s32[4,12]{1,0:T(4,128)} %bitcast.10, f32[7,7,256]{2,1,0:T(8,128)} %conv_weight.1, f32[1,256]{1,0:T(1,128)} %bitcast.11, f32[1,256]{1,0:T(1,128)} %bitcast.12, f32[1,256]{1,0:T(1,128)} %bitcast.13, ...), custom_call_target="tpu_custom_call" | custom-call | tf_op jit(solution)/shard_map/convnext_block/pallas_call | solution.py:552
  34.5 2.1 %copy.14 = bf16[12,8,16,256]{3,2,1,0:T(8,128)(2,1)} copy(bf16[12,8,16,256]{3,2,1,0:T(8,128)(2,1)} %convnext_block.1) | data formatting | bytes 1572864

commit v2 on v1

v2 whole, which is shorter than its diff:
```python
import functools

import jax
import jax.numpy as jnp
from jax import lax
from jax.experimental import pallas as pl
from jax.experimental.pallas import tpu as pltpu
from jax.sharding import PartitionSpec as P

F32, BF16 = jnp.float32, jnp.bfloat16
FACES, ROWS, COLS, CH, HID = 12, 8, 16, 256, 1024
LANES = 128
TILES, CHANS = 16, 8
STRIDE = 32
FIRST = 8
PADROWS = ROWS + 6
SIDES = 4
STRIP = FACES * 8
RELAYS = (
    (106, 77, 46, 9, 98, 69, 38, 1, 122, 93, 62, 25, 114, 85, 54, 17),
    (21, 50, 81, 118, 29, 58, 89, 126, 5, 34, 65, 102, 13, 42, 73, 110),
)


def pick(values, index):
    if len(values) == 1:
        return values[0]
    low = index % 2 == 0
    return pick([jnp.where(low, a, b) for a, b in zip(values[::2], values[1::2])], index // 2)


def relay_of(block, half):
    device = pick(RELAYS[half], block)
    return {"tile": device // CHANS, "chan": device % CHANS}


def relay_role(i, j):
    device = i * CHANS + j
    place = sum(
        jnp.where(device == relay, 1 + block + 16 * half, 0)
        for half in range(2)
        for block, relay in enumerate(RELAYS[half])
    )
    return place > 0, jnp.maximum(place - 1, 0) % 16, jnp.maximum(place - 1, 0) // 16


def each_quad(body):
    lax.fori_loop(0, FACES // 4, lambda quad, c: (body(quad), c)[1], 0)


def each_pair(body):
    lax.fori_loop(0, FACES // 2, lambda pair, c: (body(pair), c)[1], 0)


def each_face(body):
    lax.fori_loop(0, FACES, lambda face, c: (body(face), c)[1], 0)


def lanes(half):
    return pl.ds(half * LANES, LANES)


def pair_rows(pair):
    return pl.ds(pl.multiple_of(pair * 16, 16), 16)


def kernel(
    fields, neighbour, rotation, conv_weight, conv_bias, norm_gain, norm_shift,
    weight_in, bias_in, weight_out, bias_out, layer_scale,
    out,
    x, nbr, rot, cw, cb, gain, shift, w_in, b_in, w_out, b_out, scale,
    taps, padded, acc, result,
    send_left, send_right, send_edge, send_corner, columns, halo_rows, seam, corner,
    relay_in, relay_all, relay_out, relay_first, relay_last,
    local_sems, send_sems, recv_sems, out_sem,
):
    i, j = lax.axis_index("tile"), lax.axis_index("chan")
    has_up, has_down = i > 0, i < TILES - 1
    has_left, has_right = j > 0, j < CHANS - 1
    is_top, is_bottom = i == 0, i == TILES - 1
    is_left, is_right = j == 0, j == CHANS - 1
    is_relay, block, my_half = relay_role(i, j)
    turned_block = 15 - block
    odd = block % 2 == 1

    locals_ = [
        pltpu.make_async_copy(src, dst, local_sems.at[n])
        for n, (src, dst) in enumerate(
            [
                (fields, x), (neighbour, nbr), (rotation, rot), (conv_weight, cw), (conv_bias, cb),
                (norm_gain, gain), (norm_shift, shift), (weight_in, w_in), (bias_in, b_in),
                (weight_out, w_out), (bias_out, b_out), (layer_scale, scale),
            ]
        )
    ]
    for copy in locals_:
        copy.start()

    barrier = pltpu.get_barrier_semaphore()

    def greet(tile, chan):
        pl.semaphore_signal(
            barrier, inc=1, device_id={"tile": tile, "chan": chan},
            device_id_type=pl.DeviceIdType.MESH,
        )

    def greet_relays(block_):
        for half in range(2):
            there = relay_of(block_, half)
            greet(there["tile"], there["chan"])

    pl.when(has_up)(lambda: greet(i - 1, j))
    pl.when(has_down)(lambda: greet(i + 1, j))
    pl.when(has_left)(lambda: greet(i, j - 1))
    pl.when(has_right)(lambda: greet(i, j + 1))
    pl.when(has_up & has_left)(lambda: greet(i - 1, j - 1))
    pl.when(has_up & has_right)(lambda: greet(i - 1, j + 1))
    pl.when(has_down & has_left)(lambda: greet(i + 1, j - 1))
    pl.when(has_down & has_right)(lambda: greet(i + 1, j + 1))

    @pl.when(is_relay)
    def _():
        greet(0, 7 - block // 2)
        greet(block, 0)
        greet(TILES - 1, block // 2)
        greet(turned_block, CHANS - 1)

    def greet_end(to_block):
        greet_relays(to_block(2 * j))
        greet_relays(to_block(2 * j + 1))
        pl.when(has_left)(lambda: greet_relays(to_block(2 * j - 1)))
        pl.when(has_right)(lambda: greet_relays(to_block(2 * j + 2)))

    def greet_side(to_block):
        greet_relays(to_block(i))
        pl.when(has_up)(lambda: greet_relays(to_block(i - 1)))
        pl.when(has_down)(lambda: greet_relays(to_block(i + 1)))

    pl.when(is_top)(lambda: greet_end(lambda t: t))
    pl.when(is_bottom)(lambda: greet_end(lambda t: 15 - t))
    pl.when(is_left)(lambda: greet_side(lambda t: 15 - t))
    pl.when(is_right)(lambda: greet_side(lambda t: t))

    def as_int(flag):
        return flag.astype(jnp.int32)

    not_first, not_last = as_int(block > 0), as_int(block < 15)
    expected = (
        (1 + as_int(has_up) + as_int(has_down)) * (1 + as_int(has_left) + as_int(has_right)) - 1
        + 4 * as_int(is_top) + 4 * as_int(is_bottom) + 2 * as_int(is_left) + 2 * as_int(is_right)
        + as_int(is_relay)
        * (4 + 2 * (not_first + not_last) + 2 * jnp.where(odd, not_last, not_first))
    )

    locals_[0].wait()

    sublane = lax.broadcasted_iota(jnp.int32, (8, LANES), 0)

    def lower_half(a, b):
        return jnp.where(sublane < 4, a, pltpu.roll(b, 4, 0))

    def upper_half(a, b):
        return jnp.where(sublane < 4, pltpu.roll(a, 4, 0), b)

    def two(a, b):
        return jnp.concatenate([a, b], axis=0).astype(BF16)

    def pack_edge(row_of):
        def body(pair):
            for half in range(2):
                for k in range(3):
                    rows = [x[2 * pair + e, row_of(k), :, lanes(half)].astype(F32) for e in range(2)]
                    for seg in range(2):
                        send_edge[seg, half, k, pair_rows(pair), :] = two(
                            *[row[8 * seg : 8 * seg + 8] for row in rows]
                        )

        each_pair(body)

    pl.when(is_top)(lambda: pack_edge(lambda k: k))
    pl.when(is_bottom)(lambda: pack_edge(lambda k: ROWS - 1 - k))

    def unpack(face):
        for half in range(2):
            for r in range(ROWS):
                padded[face, half, pl.ds((r + 3) * STRIDE + FIRST, COLS), :] = x[
                    face, r, :, lanes(half)
                ].astype(F32)
        zero = jnp.zeros((8, LANES), F32)
        for half in range(2):
            for r in (0, 1, 2, 11, 12, 13):
                padded[face, half, pl.ds(r * STRIDE, 8), :] = zero
                padded[face, half, pl.ds(r * STRIDE + FIRST + COLS, 8), :] = zero

    each_face(unpack)

    def column(face, half, first_row, c):
        return padded[face, half, pl.ds(first_row * STRIDE + c + FIRST, 8, stride=STRIDE), :]

    def pack_columns(quad):
        for half in range(2):
            for k in range(3):
                for side, (target, c) in enumerate(((send_left, k), (send_right, COLS - 1 - k))):
                    cells = [column(4 * quad + e, half, 3, c) for e in range(4)]
                    for e in range(2):
                        target[half, k, pair_rows(2 * quad + e), :] = two(*cells[2 * e : 2 * e + 2])
                    send_corner[2 * side, half, k, pair_rows(quad), :] = two(
                        lower_half(*cells[:2]), lower_half(*cells[2:])
                    )
                    send_corner[2 * side + 1, half, k, pair_rows(quad), :] = two(
                        upper_half(*cells[:2]), upper_half(*cells[2:])
                    )

    each_quad(pack_columns)

    pl.semaphore_wait(barrier, expected)

    def remote(src, dst, send, recv, where):
        return pltpu.make_async_remote_copy(
            src_ref=src, dst_ref=dst, send_sem=send_sems.at[send], recv_sem=recv_sems.at[recv],
            device_id=where, device_id_type=pl.DeviceIdType.MESH,
        )

    COLUMNS, HALO_ROWS, SEAM, CORNER, RELAY = 0, 2, 4, 5, 9

    edge_sends = [
        (is_top, [
            remote(send_edge.at[seg, half, k], relay_in.at[k, 0], 6 * k + 2 * seg + half, RELAY + k,
                   relay_of(15 - (2 * j + seg), half))
            for k in range(3) for seg in range(2) for half in range(2)
        ]),
        (is_bottom, [
            remote(send_edge.at[seg, half, k], relay_in.at[k, 2], 6 * k + 2 * seg + half, RELAY + k,
                   relay_of(2 * j + seg, half))
            for k in range(3) for seg in range(2) for half in range(2)
        ]),
        (is_left, [
            remote(send_left.at[half, k], relay_in.at[k, 1], 6 * k + 4 + half, RELAY + k,
                   relay_of(i, half))
            for k in range(3) for half in range(2)
        ]),
        (is_right, [
            remote(send_right.at[half, k], relay_in.at[k, 3], 6 * k + 4 + half, RELAY + k,
                   relay_of(15 - i, half))
            for k in range(3) for half in range(2)
        ]),
    ]
    halo_sends = [
        (has_up, [remote(x.at[:, pl.ds(0, 3)], halo_rows.at[1], 18, HALO_ROWS + 1,
                         {"tile": i - 1, "chan": j})]),
        (has_down, [remote(x.at[:, pl.ds(ROWS - 3, 3)], halo_rows.at[0], 19, HALO_ROWS,
                           {"tile": i + 1, "chan": j})]),
        (has_left, [remote(send_left, columns.at[1], 20, COLUMNS + 1, {"tile": i, "chan": j - 1})]),
        (has_right, [remote(send_right, columns.at[0], 21, COLUMNS, {"tile": i, "chan": j + 1})]),
    ]
    for side, (there, has_side) in enumerate(((j - 1, has_left), (j + 1, has_right))):
        for end, (tile, has_end) in enumerate(((i - 1, has_up), (i + 1, has_down))):
            mine, theirs = 2 * side + end, 3 - (2 * side + end)
            halo_sends.append((
                has_side & has_end,
                [remote(send_corner.at[mine], corner.at[theirs], 22 + mine, CORNER + theirs,
                        {"tile": tile, "chan": there})],
            ))

    def relay_sends(k):
        def pass_on(source, corner_at, n, tile, chan):
            return remote(source, corner.at[corner_at, my_half, k], 26 + 10 * k + n,
                          CORNER + corner_at, {"tile": tile, "chan": chan})

        def to(side, target, n, recv, tile, chan):
            return remote(relay_out.at[k, side], target, 26 + 10 * k + n, recv,
                          {"tile": tile, "chan": chan})

        first, last = relay_first.at[k], relay_last.at[k]
        return [
            (is_relay, [
                to(0, seam.at[block % 2, my_half, k], 0, SEAM, 0, block // 2),
                to(2, seam.at[turned_block % 2, my_half, k], 1, SEAM, TILES - 1, turned_block // 2),
                to(1, columns.at[0, my_half, k], 2, COLUMNS, turned_block, 0),
                to(3, columns.at[1, my_half, k], 3, COLUMNS + 1, block, CHANS - 1),
            ]),
            (is_relay & odd & (block < 15), [
                pass_on(last.at[0], 0, 4, 0, block // 2 + 1),
                pass_on(first.at[2], 3, 5, TILES - 1, turned_block // 2 - 1),
            ]),
            (is_relay & ~odd & (block > 0), [
                pass_on(first.at[0], 2, 4, 0, block // 2 - 1),
                pass_on(last.at[2], 1, 5, TILES - 1, turned_block // 2 + 1),
            ]),
            (is_relay & (turned_block < 15), [pass_on(last.at[1], 0, 6, turned_block + 1, 0)]),
            (is_relay & (turned_block > 0), [pass_on(first.at[1], 1, 7, turned_block - 1, 0)]),
            (is_relay & (block < 15), [pass_on(last.at[3], 2, 8, block + 1, CHANS - 1)]),
            (is_relay & (block > 0), [pass_on(first.at[3], 3, 9, block - 1, CHANS - 1)]),
        ]

    def start_all(sends):
        for condition, copies in sends:
            @pl.when(condition)
            def _():
                for copy in copies:
                    copy.start()

    def arrived(buffer, recv):
        pltpu.make_async_copy(buffer, buffer, recv_sems.at[recv]).wait()

    start_all(edge_sends)
    start_all(halo_sends)

    locals_[3].wait()
    locals_[4].wait()
    for half in range(2):
        for a in range(7):
            for b in range(7):
                taps[half, a * 7 + b] = jnp.broadcast_to(cw[a, pl.ds(b, 1), lanes(half)], (8, LANES))

    def convolve(face, half, group, total, rows, shifts):
        for b in shifts:
            cells = {
                r: padded[face, half, pl.ds(r * STRIDE + FIRST - 3 + b + 8 * group, 8), :]
                for r in rows
            }
            for a in range(7):
                tap = taps[half, a * 7 + b]
                for r in range(ROWS):
                    if r + a in cells and r in total:
                        total[r] = total[r] + tap * cells[r + a]
        return total

    own = range(3, 11)
    near = (range(3, 7), range(4))
    far = (range(3), range(4, 7))

    def add_taps(side, out_rows, rows, shifts, first=False):
        def body(face):
            for half in range(2):
                if first:
                    bias = jnp.broadcast_to(cb[:, lanes(half)], (8, LANES))
                    total = {r: bias for r in out_rows}
                else:
                    total = {r: acc[side, r, face, :, lanes(half)] for r in out_rows}
                for r, value in convolve(face, half, side, total, rows, shifts).items():
                    acc[side, r, face, :, lanes(half)] = value

        each_face(body)

    for side in range(2):
        add_taps(side, range(ROWS), own, near[side], first=True)

    locals_[1].wait()
    locals_[2].wait()

    @pl.when(is_relay)
    def _():
        row = lax.broadcasted_iota(jnp.int32, (STRIP, STRIP), 0)
        col = lax.broadcasted_iota(jnp.int32, (STRIP, STRIP), 1)
        turn = (row // 8 * 8 + 7 - row % 8 == col).astype(BF16)

        def relay(k, carry):
            arrived(relay_in.at[k], RELAY + k)
            for side in range(SIDES):
                strip = relay_in[k, side]
                at = pl.ds(side * FACES, FACES)
                relay_all[0, at] = strip.astype(F32).reshape(FACES, 8, LANES)
                relay_all[1, at] = jnp.dot(turn, strip, preferred_element_type=F32).reshape(
                    FACES, 8, LANES
                )

            def choose(quad):
                for side in range(SIDES):
                    cells = []
                    for e in range(4):
                        source = (side + 6 - rot[side, 4 * quad + e]) & 3
                        same = ((source + 1) & 3) >> 1
                        flip = same if side in (1, 2) else 1 - same
                        cells.append(relay_all[flip, source * FACES + nbr[side, 4 * quad + e]])
                    for e in range(2):
                        relay_out[k, side, pair_rows(2 * quad + e), :] = two(
                            *cells[2 * e : 2 * e + 2]
                        )
                    relay_first[k, side, pair_rows(quad), :] = two(
                        lower_half(*cells[:2]), lower_half(*cells[2:])
                    )
                    relay_last[k, side, pair_rows(quad), :] = two(
                        upper_half(*cells[:2]), upper_half(*cells[2:])
                    )

            each_quad(choose)
            start_all(relay_sends(k))
            return carry

        lax.fori_loop(0, 3, relay, 0)

    def unpack_rows(end, first_row):
        def body(face):
            for half in range(2):
                for r in range(3):
                    padded[face, half, pl.ds((first_row + r) * STRIDE + FIRST, COLS), :] = halo_rows[
                        end, face, r, :, lanes(half)
                    ].astype(F32)

        each_face(body)

    def unpack_seam(row_of):
        def body(pair):
            for half in range(2):
                for seg in range(2):
                    for k in range(3):
                        both = seam[seg, half, k, pair_rows(pair), :].astype(F32)
                        for e in range(2):
                            padded[
                                2 * pair + e, half, pl.ds(row_of(k) * STRIDE + FIRST + 8 * seg, 8), :
                            ] = both[8 * e : 8 * e + 8]

        each_pair(body)

    def unpack_columns(side):
        def body(pair):
            for half in range(2):
                for k in range(3):
                    both = columns[side, half, k, pair_rows(pair), :].astype(F32)
                    col = -1 - k if side == 0 else COLS + k
                    for e in range(2):
                        padded[
                            2 * pair + e, half,
                            pl.ds(3 * STRIDE + FIRST + col, 8, stride=STRIDE), :
                        ] = both[8 * e : 8 * e + 8]

        each_pair(body)

    def unpack_corner(at, beside, end):
        first_col = -4 if at < 2 else COLS

        def body(quad):
            for half in range(2):
                for k in range(3):
                    cells = corner[at, half, k, pair_rows(quad), :].astype(F32)
                    for e in range(4):
                        if beside:
                            col = -1 - k if at < 2 else COLS + k
                            first, row = (1, 0) if end == 0 else (0, 11)
                            padded[
                                4 * quad + e, half,
                                pl.ds(row * STRIDE + FIRST + col, 3, stride=STRIDE), :
                            ] = cells[4 * e + first : 4 * e + first + 3]
                        else:
                            row = 2 - k if end == 0 else 11 + k
                            padded[
                                4 * quad + e, half, pl.ds(row * STRIDE + FIRST + first_col, 4), :
                            ] = cells[4 * e : 4 * e + 4]

        each_quad(body)

    by_columns = is_left | is_right
    late = (is_left, is_right)
    first_end = as_int(is_top)

    def take_rows(end):
        at_end = (is_top, is_bottom)[end]

        @pl.when(~at_end)
        def _():
            arrived(halo_rows.at[end], HALO_ROWS + end)
            unpack_rows(end, 11 * end)

        @pl.when(at_end)
        def _():
            arrived(seam, SEAM)
            unpack_seam((lambda k: 2 - k) if end == 0 else (lambda k: 11 + k))

    def take_columns(side):
        arrived(columns.at[side], COLUMNS + side)
        unpack_columns(side)
        add_taps(side, range(ROWS), own, far[side])

    def take_corner(end, side):
        at = 2 * side + end
        has_side, has_end = (has_left, has_right)[side], (has_up, has_down)[end]

        @pl.when(has_side | has_end)
        def _():
            arrived(corner.at[at], CORNER + at)

        pl.when(has_end)(functools.partial(unpack_corner, at, True, end))
        pl.when(~has_end & has_side)(functools.partial(unpack_corner, at, False, end))

    def add_end(end, side, shifts):
        if end == 0:
            add_taps(side, range(3), range(3), shifts)
        else:
            add_taps(side, range(5, 8), range(11, 14), shifts)

    for copy in locals_[5:]:
        copy.wait()

    def pointwise(at):
        cells = acc.at[at]
        shape = cells.shape
        values = cells[...].reshape(-1, CH).astype(BF16).astype(F32)
        mean = jnp.mean(values, axis=-1, keepdims=True)
        apart = values - mean
        spread = jnp.mean(apart * apart, axis=-1, keepdims=True)
        normed = (apart * lax.rsqrt(spread + 1e-6) * gain[...] + shift[...]).astype(BF16)
        hidden = jnp.dot(normed, w_in[...], preferred_element_type=F32) + b_in[...]
        inner_ = hidden * (0.7978845608028654 + 0.035677408136300125 * (hidden * hidden))
        hidden = (hidden * (1.0 + jnp.tanh(inner_))).astype(BF16)
        update = 0.5 * jnp.dot(hidden, w_out[...], preferred_element_type=F32) + b_out[...]
        cells[...] = (scale[...] * update).reshape(shape)

    def finish(first, count):
        def body(face):
            for r in range(count):
                row = first + r
                for half in range(2):
                    update = jnp.concatenate(
                        [acc[side, row, face, :, lanes(half)] for side in range(2)], axis=0
                    )
                    result[face, row, :, lanes(half)] = (
                        x[face, row, :, lanes(half)].astype(F32) + update
                    ).astype(BF16)
            rows = pl.ds(first, count)
            pltpu.make_async_copy(result.at[face, rows], out.at[face, rows], out_sem).start()

        each_face(body)

    both = pl.ds(0, 2)
    early_side = as_int(is_left)

    for side in range(2):
        pl.when(~late[side])(functools.partial(take_columns, side))

    @pl.when(~by_columns)
    def _():
        pointwise((both, pl.ds(3, 2)))
        finish(3, 2)

    def take_end(n, carry):
        end = (first_end + n) % 2
        for an_end in range(2):
            @pl.when(end == an_end)
            def _():
                take_rows(an_end)
                for side in range(2):
                    @pl.when(~late[side])
                    def _():
                        take_corner(an_end, side)
                        add_end(an_end, side, range(7))

                    @pl.when(late[side])
                    def _():
                        add_end(an_end, side, near[side])

        @pl.when(~by_columns)
        def _():
            pointwise((both, pl.ds(5 * end, 3)))
            finish(5 * end, 3)

        @pl.when(by_columns)
        def _():
            pointwise((early_side, pl.ds(4 * end, 4)))

        return carry

    lax.fori_loop(0, 2, take_end, 0)

    for side in range(2):
        @pl.when(late[side])
        def _():
            take_columns(side)
            for end in range(2):
                take_corner(end, side)
                add_end(end, side, far[side])

    @pl.when(by_columns)
    def _():
        def last(end, carry):
            pointwise((1 - early_side, pl.ds(4 * end, 4)))
            finish(4 * end, 4)
            return carry

        lax.fori_loop(0, 2, last, 0)

    pltpu.make_async_copy(result, out, out_sem).wait()

    for condition, copies in edge_sends + halo_sends:
        @pl.when(condition)
        def _():
            for copy in copies:
                copy.wait_send()

    for k in range(3):
        for condition, copies in relay_sends(k):
            @pl.when(condition)
            def _():
                for copy in copies:
                    copy.wait_send()


def block(fields, neighbour, rotation, conv_weight, conv_bias, norm_gain, norm_shift,
          weight_in, bias_in, weight_out, bias_out, layer_scale):
    def row(vector):
        return vector.reshape(1, -1)

    anywhere = pl.BlockSpec(memory_space=pl.ANY)
    strip = pltpu.VMEM((2, 3, STRIP, LANES), BF16)
    corners = pltpu.VMEM((4, 2, 3, STRIP // 2, LANES), BF16)
    relayed = pltpu.VMEM((3, SIDES, STRIP, LANES), BF16)
    relayed_half = pltpu.VMEM((3, SIDES, STRIP // 2, LANES), BF16)
    return pl.pallas_call(
        kernel,
        out_shape=jax.ShapeDtypeStruct(fields.shape, BF16),
        in_specs=[anywhere] * 12,
        out_specs=anywhere,
        scratch_shapes=[
            pltpu.VMEM(fields.shape, BF16),
            pltpu.SMEM((SIDES, FACES), jnp.int32),
            pltpu.SMEM((SIDES, FACES), jnp.int32),
            pltpu.VMEM((7, 7, CH), F32),
            pltpu.VMEM((1, CH), F32),
            pltpu.VMEM((1, CH), F32),
            pltpu.VMEM((1, CH), F32),
            pltpu.VMEM((CH, HID), BF16),
            pltpu.VMEM((1, HID), F32),
            pltpu.VMEM((HID, CH), BF16),
            pltpu.VMEM((1, CH), F32),
            pltpu.VMEM((1, CH), F32),
            pltpu.VMEM((2, 49, 8, LANES), F32),
            pltpu.VMEM((FACES, 2, PADROWS * STRIDE, LANES), F32),
            pltpu.VMEM((2, ROWS, FACES, 8, CH), F32),
            pltpu.VMEM(fields.shape, BF16),
            strip, strip,
            pltpu.VMEM((2, 2, 3, STRIP, LANES), BF16),
            corners,
            pltpu.VMEM((2, 2, 3, STRIP, LANES), BF16),
            pltpu.VMEM((2, FACES, 3, COLS, CH), BF16),
            pltpu.VMEM((2, 2, 3, STRIP, LANES), BF16),
            corners,
            relayed,
            pltpu.VMEM((2, SIDES * FACES, 8, LANES), F32),
            relayed, relayed_half, relayed_half,
            pltpu.SemaphoreType.DMA((12,)),
            pltpu.SemaphoreType.DMA((56,)),
            pltpu.SemaphoreType.DMA((12,)),
            pltpu.SemaphoreType.DMA,
        ],
        compiler_params=pltpu.CompilerParams(
            collective_id=0, has_side_effects=True, vmem_limit_bytes=63 * 2**20
        ),
        name="convnext_block",
    )(
        fields, neighbour.T, rotation.T, conv_weight, row(conv_bias), row(norm_gain), row(norm_shift),
        weight_in, row(bias_in), weight_out, row(bias_out), row(layer_scale),
    )


def solution(mesh):
    cells = P(None, "tile", "chan", None)
    return jax.shard_map(
        block, mesh=mesh, in_specs=(cells,) + (P(),) * 11, out_specs=cells, check_vma=False
    )
```

time: 36.7 us -> 32.8 us (0.89)
  the two profiles are of different devices: /device:TPU:2 before, /device:TPU:0 now
where the time goes in v2:
time: 32.8 us; the launch traced here: 32.6 us
  Pallas kernels  30.5 us (93%)
  local copies, waits for them, and re-layouts  2.06 us (6%)
    pallas_call x1, Pallas kernels, block(): pl.pallas_call(kernel, out_shape=jax.ShapeDtypeStruct(fields.shape, BF16)...  30.5 us
    unnamed x1, local copies, waits for them, and re-layouts  2.06 us

profile of v2, /device:TPU:0, one launch (start us, length us, event | category | flops | bytes accessed | tf_op | source)
XLA Modules:
  0.0 32.6 jit_solution(16478290463268508653)
XLA Ops:
  0.0 30.5 %convnext_block.1 = bf16[12,8,16,256]{3,2,1,0:T(8,128)(2,1)} custom-call(bf16[12,8,16,256]{3,2,1,0:T(8,128)(2,1)} %fields.1, s32[4,12]{1,0:T(4,128)} %bitcast.9, s32[4,12]{1,0:T(4,128)} %bitcast.10, f32[7,7,256]{2,1,0:T(8,128)} %conv_weight.1, f32[1,256]{1,0:T(1,128)} %bitcast.11, f32[1,256]{1,0:T(1,128)} %bitcast.12, f32[1,256]{1,0:T(1,128)} %bitcast.13, ...), custom_call_target="tpu_custom_call" | custom-call | tf_op jit(solution)/shard_map/convnext_block/pallas_call | solution.py:608
  30.6 2.1 %copy.14 = bf16[12,8,16,256]{3,2,1,0:T(8,128)(2,1)} copy(bf16[12,8,16,256]{3,2,1,0:T(8,128)(2,1)} %convnext_block.1) | data formatting | bytes 1572864

commit v3 on v2

--- a/solution.py
+++ b/solution.py
@@ -17,8 +17,8 @@
 SIDES = 4
 STRIP = FACES * 8
 RELAYS = (
-    (106, 77, 46, 9, 98, 69, 38, 1, 122, 93, 62, 25, 114, 85, 54, 17),
-    (21, 50, 81, 118, 29, 58, 89, 126, 5, 34, 65, 102, 13, 42, 73, 110),
+    (25, 106, 9, 102, 36, 58, 105, 92, 90, 84, 50, 28, 14, 113, 118, 101),
+    (70, 22, 114, 62, 100, 66, 12, 65, 34, 10, 20, 38, 30, 17, 97, 57),
 )
 
 
@@ -69,8 +69,8 @@
     weight_in, bias_in, weight_out, bias_out, layer_scale,
     out,
     x, nbr, rot, cw, cb, gain, shift, w_in, b_in, w_out, b_out, scale,
-    taps, padded, acc, result,
-    send_left, send_right, send_edge, send_corner, columns, halo_rows, seam, corner,
+    taps, padded, acc, kept, patch, result,
+    send_left, send_right, send_edge, send_ends, columns, halo_rows, seam, corner, ends_in,
     relay_in, relay_all, relay_out, relay_first, relay_last,
     local_sems, send_sems, recv_sems, out_sem,
 ):
@@ -93,8 +93,7 @@
             ]
         )
     ]
-    for copy in locals_:
-        copy.start()
+    locals_[0].start()
 
     barrier = pltpu.get_barrier_semaphore()
 
@@ -108,15 +107,6 @@
         for half in range(2):
             there = relay_of(block_, half)
             greet(there["tile"], there["chan"])
-
-    pl.when(has_up)(lambda: greet(i - 1, j))
-    pl.when(has_down)(lambda: greet(i + 1, j))
-    pl.when(has_left)(lambda: greet(i, j - 1))
-    pl.when(has_right)(lambda: greet(i, j + 1))
-    pl.when(has_up & has_left)(lambda: greet(i - 1, j - 1))
-    pl.when(has_up & has_right)(lambda: greet(i - 1, j + 1))
-    pl.when(has_down & has_left)(lambda: greet(i + 1, j - 1))
-    pl.when(has_down & has_right)(lambda: greet(i + 1, j + 1))
 
     @pl.when(is_relay)
     def _():
@@ -141,12 +131,19 @@
     pl.when(is_left)(lambda: greet_side(lambda t: 15 - t))
     pl.when(is_right)(lambda: greet_side(lambda t: t))
 
+    pl.when(has_up)(lambda: greet(i - 1, j))
+    pl.when(has_down)(lambda: greet(i + 1, j))
+    pl.when(has_left)(lambda: greet(i, j - 1))
+    pl.when(has_right)(lambda: greet(i, j + 1))
+    for copy in locals_[1:]:
+        copy.start()
+
     def as_int(flag):
         return flag.astype(jnp.int32)
 
     not_first, not_last = as_int(block > 0), as_int(block < 15)
     expected = (
-        (1 + as_int(has_up) + as_int(has_down)) * (1 + as_int(has_left) + as_int(has_right)) - 1
+        as_int(has_up) + as_int(has_down) + as_int(has_left) + as_int(has_right)
         + 4 * as_int(is_top) + 4 * as_int(is_bottom) + 2 * as_int(is_left) + 2 * as_int(is_right)
         + as_int(is_relay)
         * (4 + 2 * (not_first + not_last) + 2 * jnp.where(odd, not_last, not_first))
@@ -194,22 +191,28 @@
 
     each_face(unpack)
 
+    @pl.when(is_left | is_right)
+    def _():
+        def clear(face):
+            for half in range(2):
+                for r in range(3, 11):
+                    for c in (-FIRST, COLS):
+                        padded[face, half, pl.ds(r * STRIDE + FIRST + c, 8), :] = jnp.zeros(
+                            (8, LANES), F32
+                        )
+
+        each_face(clear)
+
     def column(face, half, first_row, c):
         return padded[face, half, pl.ds(first_row * STRIDE + c + FIRST, 8, stride=STRIDE), :]
 
     def pack_columns(quad):
         for half in range(2):
             for k in range(3):
-                for side, (target, c) in enumerate(((send_left, k), (send_right, COLS - 1 - k))):
+                for target, c in ((send_left, k), (send_right, COLS - 1 - k)):
                     cells = [column(4 * quad + e, half, 3, c) for e in range(4)]
                     for e in range(2):
                         target[half, k, pair_rows(2 * quad + e), :] = two(*cells[2 * e : 2 * e + 2])
-                    send_corner[2 * side, half, k, pair_rows(quad), :] = two(
-                        lower_half(*cells[:2]), lower_half(*cells[2:])
-                    )
-                    send_corner[2 * side + 1, half, k, pair_rows(quad), :] = two(
-                        upper_half(*cells[:2]), upper_half(*cells[2:])
-                    )
 
     each_quad(pack_columns)
 
@@ -221,7 +224,7 @@
             device_id=where, device_id_type=pl.DeviceIdType.MESH,
         )
 
-    COLUMNS, HALO_ROWS, SEAM, CORNER, RELAY = 0, 2, 4, 5, 9
+    COLUMNS, HALO_ROWS, SEAM, CORNER, RELAY, ENDS = 0, 2, 4, 5, 9, 12
 
     edge_sends = [
         (is_top, [
@@ -253,22 +256,18 @@
         (has_left, [remote(send_left, columns.at[1], 20, COLUMNS + 1, {"tile": i, "chan": j - 1})]),
         (has_right, [remote(send_right, columns.at[0], 21, COLUMNS, {"tile": i, "chan": j + 1})]),
     ]
-    for side, (there, has_side) in enumerate(((j - 1, has_left), (j + 1, has_right))):
-        for end, (tile, has_end) in enumerate(((i - 1, has_up), (i + 1, has_down))):
-            mine, theirs = 2 * side + end, 3 - (2 * side + end)
-            halo_sends.append((
-                has_side & has_end,
-                [remote(send_corner.at[mine], corner.at[theirs], 22 + mine, CORNER + theirs,
-                        {"tile": tile, "chan": there})],
-            ))
+    end_sends = [
+        (has_left, [remote(send_ends.at[0], ends_in.at[1], 22, ENDS + 1, {"tile": i, "chan": j - 1})]),
+        (has_right, [remote(send_ends.at[1], ends_in.at[0], 23, ENDS, {"tile": i, "chan": j + 1})]),
+    ]
 
     def relay_sends(k):
         def pass_on(source, corner_at, n, tile, chan):
-            return remote(source, corner.at[corner_at, my_half, k], 26 + 10 * k + n,
+            return remote(source, corner.at[corner_at, my_half, k], 24 + 10 * k + n,
                           CORNER + corner_at, {"tile": tile, "chan": chan})
 
         def to(side, target, n, recv, tile, chan):
-            return remote(relay_out.at[k, side], target, 26 + 10 * k + n, recv,
+            return remote(relay_out.at[k, side], target, 24 + 10 * k + n, recv,
                           {"tile": tile, "chan": chan})
 
         first, last = relay_first.at[k], relay_last.at[k]
@@ -346,6 +345,172 @@
     for side in range(2):
         add_taps(side, range(ROWS), own, near[side], first=True)
 
+    def unpack_rows(end, first_row):
+        def body(face):
+            for half in range(2):
+                for r in range(3):
+                    padded[face, half, pl.ds((first_row + r) * STRIDE + FIRST, COLS), :] = halo_rows[
+                        end, face, r, :, lanes(half)
+                    ].astype(F32)
+
+        each_face(body)
+
+    def unpack_seam(row_of):
+        def body(pair):
+            for half in range(2):
+                for seg in range(2):
+                    for k in range(3):
+                        both = seam[seg, half, k, pair_rows(pair), :].astype(F32)
+                        for e in range(2):
+                            padded[
+                                2 * pair + e, half, pl.ds(row_of(k) * STRIDE + FIRST + 8 * seg, 8), :
+                            ] = both[8 * e : 8 * e + 8]
+
+        each_pair(body)
+
+    def unpack_columns(side):
+        def body(pair):
+            for half in range(2):
+                for k in range(3):
+                    both = columns[side, half, k, pair_rows(pair), :].astype(F32)
+                    col = -1 - k if side == 0 else COLS + k
+                    for e in range(2):
+                        padded[
+                            2 * pair + e, half,
+                            pl.ds(3 * STRIDE + FIRST + col, 8, stride=STRIDE), :
+                        ] = both[8 * e : 8 * e + 8]
+
+        each_pair(body)
+
+    def unpack_corner(at, beside, end):
+        first_col = -4 if at < 2 else COLS
+
+        def body(quad):
+            for half in range(2):
+                for k in range(3):
+                    cells = corner[at, half, k, pair_rows(quad), :].astype(F32)
+                    for e in range(4):
+                        if beside:
+                            col = -1 - k if at < 2 else COLS + k
+                            first, row = (1, 0) if end == 0 else (0, 11)
+                            padded[
+                                4 * quad + e, half,
+                                pl.ds(row * STRIDE + FIRST + col, 3, stride=STRIDE), :
+                            ] = cells[4 * e + first : 4 * e + first + 3]
+                        else:
+                            row = 2 - k if end == 0 else 11 + k
+                            padded[
+                                4 * quad + e, half, pl.ds(row * STRIDE + FIRST + first_col, 4), :
+                            ] = cells[4 * e : 4 * e + 4]
+
+        each_quad(body)
+
+    late = (is_left, is_right)
+    any_late = is_left | is_right
+    first_end = as_int(is_top)
+
+    def take_rows(end):
+        arrived(halo_rows.at[end], HALO_ROWS + end)
+        unpack_rows(end, 11 * end)
+
+    def take_seam(end):
+        arrived(seam, SEAM)
+        unpack_seam((lambda k: 2 - k) if end == 0 else (lambda k: 11 + k))
+
+    def pack_ends(quad):
+        for half in range(2):
+            for k in range(3):
+                for side in range(2):
+                    c = k if side == 0 else COLS - 1 - k
+                    cells = [
+                        jnp.where(
+                            sublane < 4,
+                            column(4 * quad + e, half, 0, c),
+                            column(4 * quad + e, half, 6, c),
+                        )
+                        for e in range(4)
+                    ]
+                    for e in range(2):
+                        send_ends[side, half, k, pair_rows(2 * quad + e), :] = two(
+                            *cells[2 * e : 2 * e + 2]
+                        )
+
+    def unpack_ends(side, end):
+        def body(pair):
+            for half in range(2):
+                for k in range(3):
+                    cells = ends_in[side, half, k, pair_rows(pair), :].astype(F32)
+                    col = -1 - k if side == 0 else COLS + k
+                    for e in range(2):
+                        first = 8 * e + 5 * end
+                        padded[
+                            2 * pair + e, half,
+                            pl.ds(11 * end * STRIDE + FIRST + col, 3, stride=STRIDE), :
+                        ] = cells[first : first + 3]
+
+        each_pair(body)
+
+    def take_columns(side):
+        arrived(columns.at[side], COLUMNS + side)
+        unpack_columns(side)
+
+    def take_corner(end, side, beside):
+        at = 2 * side + end
+        arrived(corner.at[at], CORNER + at)
+        unpack_corner(at, beside, end)
+
+    def add_end(end, side, shifts):
+        if end == 0:
+            add_taps(side, range(3), range(3), shifts)
+        else:
+            add_taps(side, range(5, 8), range(11, 14), shifts)
+
+    for copy in locals_[5:]:
+        copy.wait()
+
+    def pointwise(cells):
+        shape = cells.shape
+        values = cells[...].reshape(-1, CH).astype(BF16).astype(F32)
+        mean = jnp.mean(values, axis=-1, keepdims=True)
+        apart = values - mean
+        spread = jnp.mean(apart * apart, axis=-1, keepdims=True)
+        normed = (apart * lax.rsqrt(spread + 1e-6) * gain[...] + shift[...]).astype(BF16)
+        hidden = jnp.dot(normed, w_in[...], preferred_element_type=F32) + b_in[...]
+        inner_ = hidden * (0.7978845608028654 + 0.035677408136300125 * (hidden * hidden))
+        hidden = (hidden * (1.0 + jnp.tanh(inner_))).astype(BF16)
+        update = 0.5 * jnp.dot(hidden, w_out[...], preferred_element_type=F32) + b_out[...]
+        cells[...] = (scale[...] * update).reshape(shape)
+
+    def finish(first, count):
+        def body(face):
+            for r in range(count):
+                row = first + r
+                for half in range(2):
+                    update = jnp.concatenate(
+                        [acc[side, row, face, :, lanes(half)] for side in range(2)], axis=0
+                    )
+                    result[face, row, :, lanes(half)] = (
+                        x[face, row, :, lanes(half)].astype(F32) + update
+                    ).astype(BF16)
+            rows = pl.ds(first, count)
+            pltpu.make_async_copy(result.at[face, rows], out.at[face, rows], out_sem).start()
+
+        each_face(body)
+
+    def keep(side, rows):
+        def body(face):
+            for r in rows:
+                for half in range(2):
+                    kept[half, face, pl.ds(8 * r, 8), :] = acc[side, r, face, :, lanes(half)]
+
+        each_face(body)
+
+    both = pl.ds(0, 2)
+
+    for side in range(2):
+        pl.when(~late[side])(functools.partial(take_columns, side))
+        add_taps(side, range(ROWS), own, far[side])
+
     locals_[1].wait()
     locals_[2].wait()
 
@@ -390,198 +555,116 @@
 
         lax.fori_loop(0, 3, relay, 0)
 
-    def unpack_rows(end, first_row):
-        def body(face):
-            for half in range(2):
-                for r in range(3):
-                    padded[face, half, pl.ds((first_row + r) * STRIDE + FIRST, COLS), :] = halo_rows[
-                        end, face, r, :, lanes(half)
-                    ].astype(F32)
-
-        each_face(body)
-
-    def unpack_seam(row_of):
-        def body(pair):
-            for half in range(2):
-                for seg in range(2):
-                    for k in range(3):
-                        both = seam[seg, half, k, pair_rows(pair), :].astype(F32)
-                        for e in range(2):
-                            padded[
-                                2 * pair + e, half, pl.ds(row_of(k) * STRIDE + FIRST + 8 * seg, 8), :
-                            ] = both[8 * e : 8 * e + 8]
-
-        each_pair(body)
-
-    def unpack_columns(side):
-        def body(pair):
-            for half in range(2):
-                for k in range(3):
-                    both = columns[side, half, k, pair_rows(pair), :].astype(F32)
-                    col = -1 - k if side == 0 else COLS + k
-                    for e in range(2):
-                        padded[
-                            2 * pair + e, half,
-                            pl.ds(3 * STRIDE + FIRST + col, 8, stride=STRIDE), :
-                        ] = both[8 * e : 8 * e + 8]
-
-        each_pair(body)
-
-    def unpack_corner(at, beside, end):
-        first_col = -4 if at < 2 else COLS
-
-        def body(quad):
-            for half in range(2):
-                for k in range(3):
-                    cells = corner[at, half, k, pair_rows(quad), :].astype(F32)
-                    for e in range(4):
-                        if beside:
-                            col = -1 - k if at < 2 else COLS + k
-                            first, row = (1, 0) if end == 0 else (0, 11)
-                            padded[
-                                4 * quad + e, half,
-                                pl.ds(row * STRIDE + FIRST + col, 3, stride=STRIDE), :
-                            ] = cells[4 * e + first : 4 * e + first + 3]
-                        else:
-                            row = 2 - k if end == 0 else 11 + k
-                            padded[
-                                4 * quad + e, half, pl.ds(row * STRIDE + FIRST + first_col, 4), :
-                            ] = cells[4 * e : 4 * e + 4]
-
-        each_quad(body)
-
-    by_columns = is_left | is_right
-    late = (is_left, is_right)
-    first_end = as_int(is_top)
-
-    def take_rows(end):
-        at_end = (is_top, is_bottom)[end]
-
-        @pl.when(~at_end)
+    for side in range(2):
+        pl.when(late[side])(functools.partial(keep, side, range(3, 5)))
+    pointwise(acc.at[both, pl.ds(3, 2)])
+    pl.when(~any_late)(functools.partial(finish, 3, 2))
+
+    for end in range(2):
+        pl.when((has_up, has_down)[end])(functools.partial(take_rows, end))
+    each_quad(pack_ends)
+    start_all(end_sends)
+    for end in range(2):
+        @pl.when((has_up, has_down)[end])
         def _():
-            arrived(halo_rows.at[end], HALO_ROWS + end)
-            unpack_rows(end, 11 * end)
-
-        @pl.when(at_end)
+            for side in range(2):
+                add_end(end, side, near[side])
+
+    for side in range(2):
+        @pl.when((has_left, has_right)[side])
         def _():
-            arrived(seam, SEAM)
-            unpack_seam((lambda k: 2 - k) if end == 0 else (lambda k: 11 + k))
-
-    def take_columns(side):
-        arrived(columns.at[side], COLUMNS + side)
-        unpack_columns(side)
-        add_taps(side, range(ROWS), own, far[side])
-
-    def take_corner(end, side):
-        at = 2 * side + end
-        has_side, has_end = (has_left, has_right)[side], (has_up, has_down)[end]
-
-        @pl.when(has_side | has_end)
-        def _():
-            arrived(corner.at[at], CORNER + at)
-
-        pl.when(has_end)(functools.partial(unpack_corner, at, True, end))
-        pl.when(~has_end & has_side)(functools.partial(unpack_corner, at, False, end))
-
-    def add_end(end, side, shifts):
-        if end == 0:
-            add_taps(side, range(3), range(3), shifts)
-        else:
-            add_taps(side, range(5, 8), range(11, 14), shifts)
-
-    for copy in locals_[5:]:
-        copy.wait()
-
-    def pointwise(at):
-        cells = acc.at[at]
-        shape = cells.shape
-        values = cells[...].reshape(-1, CH).astype(BF16).astype(F32)
-        mean = jnp.mean(values, axis=-1, keepdims=True)
-        apart = values - mean
-        spread = jnp.mean(apart * apart, axis=-1, keepdims=True)
-        normed = (apart * lax.rsqrt(spread + 1e-6) * gain[...] + shift[...]).astype(BF16)
-        hidden = jnp.dot(normed, w_in[...], preferred_element_type=F32) + b_in[...]
-        inner_ = hidden * (0.7978845608028654 + 0.035677408136300125 * (hidden * hidden))
-        hidden = (hidden * (1.0 + jnp.tanh(inner_))).astype(BF16)
-        update = 0.5 * jnp.dot(hidden, w_out[...], preferred_element_type=F32) + b_out[...]
-        cells[...] = (scale[...] * update).reshape(shape)
-
-    def finish(first, count):
-        def body(face):
-            for r in range(count):
-                row = first + r
-                for half in range(2):
-                    update = jnp.concatenate(
-                        [acc[side, row, face, :, lanes(half)] for side in range(2)], axis=0
-                    )
-                    result[face, row, :, lanes(half)] = (
-                        x[face, row, :, lanes(half)].astype(F32) + update
-                    ).astype(BF16)
-            rows = pl.ds(first, count)
-            pltpu.make_async_copy(result.at[face, rows], out.at[face, rows], out_sem).start()
-
-        each_face(body)
-
-    both = pl.ds(0, 2)
-    early_side = as_int(is_left)
-
-    for side in range(2):
-        pl.when(~late[side])(functools.partial(take_columns, side))
-
-    @pl.when(~by_columns)
-    def _():
-        pointwise((both, pl.ds(3, 2)))
-        finish(3, 2)
+            arrived(ends_in.at[side], ENDS + side)
+            for end in range(2):
+                pl.when((has_up, has_down)[end])(functools.partial(unpack_ends, side, end))
 
     def take_end(n, carry):
         end = (first_end + n) % 2
         for an_end in range(2):
+            at_end = (is_top, is_bottom)[an_end]
+
+            @pl.when((end == an_end) & ~at_end)
+            def _():
+                for side in range(2):
+                    add_end(an_end, side, far[side])
+
+            @pl.when((end == an_end) & at_end)
+            def _():
+                take_seam(an_end)
+                for side in range(2):
+                    pl.when((has_left, has_right)[side])(
+                        functools.partial(take_corner, an_end, side, False)
+                    )
+                    add_end(an_end, side, range(7))
+
             @pl.when(end == an_end)
             def _():
-                take_rows(an_end)
                 for side in range(2):
-                    @pl.when(~late[side])
-                    def _():
-                        take_corner(an_end, side)
-                        add_end(an_end, side, range(7))
-
-                    @pl.when(late[side])
-                    def _():
-                        add_end(an_end, side, near[side])
-
-        @pl.when(~by_columns)
-        def _():
-            pointwise((both, pl.ds(5 * end, 3)))
-            finish(5 * end, 3)
-
-        @pl.when(by_columns)
-        def _():
-            pointwise((early_side, pl.ds(4 * end, 4)))
-
+                    pl.when(late[side])(
+                        functools.partial(keep, side, range(3) if an_end == 0 else range(5, 8))
+                    )
+
+        pointwise(acc.at[both, pl.ds(5 * end, 3)])
+        pl.when(~any_late)(lambda: finish(5 * end, 3))
         return carry
 
     lax.fori_loop(0, 2, take_end, 0)
+
+    def add_columns(side):
+        def body(face):
+            for half in range(2):
+                cells = [
+                    [column(face, half, a, -1 - k if side == 0 else COLS + k) for a in range(7)]
+                    for k in range(3)
+                ]
+                for n in range(3):
+                    c = n if side == 0 else 5 + n
+                    total = kept[half, face, pl.ds(c, ROWS, stride=8), :]
+                    for b in range(3 - n) if side == 0 else range(6 - n, 7):
+                        k = 2 - b - n if side == 0 else n + b - 6
+                        for a in range(7):
+                            total = total + taps[half, a * 7 + b] * cells[k][a]
+                    patch[n, face, :, lanes(half)] = total
+
+        each_face(body)
+
+    def put_columns(side):
+        def body(face):
+            for half in range(2):
+                for n in range(3):
+                    c = n if side == 0 else 5 + n
+                    kept[half, face, pl.ds(c, ROWS, stride=8), :] = patch[n, face, :, lanes(half)]
+            near_seam = sublane < 3 if side == 0 else sublane > 4
+            for row in range(ROWS):
+                for half in range(2):
+                    update = [acc[a_side, row, face, :, lanes(half)] for a_side in range(2)]
+                    update[side] = jnp.where(
+                        near_seam, kept[half, face, pl.ds(8 * row, 8), :], update[side]
+                    )
+                    result[face, row, :, lanes(half)] = (
+                        x[face, row, :, lanes(half)].astype(F32) + jnp.concatenate(update, axis=0)
+                    ).astype(BF16)
+            pltpu.make_async_copy(result.at[face], out.at[face], out_sem).start()
+
+        each_face(body)
 
     for side in range(2):
         @pl.when(late[side])
         def _():
             take_columns(side)
             for end in range(2):
-                take_corner(end, side)
-                add_end(end, side, far[side])
-
-    @pl.when(by_columns)
+                pl.when((has_up, has_down)[end])(functools.partial(take_corner, end, side, True))
+            add_columns(side)
+
+    @pl.when(any_late)
     def _():
-        def last(end, carry):
-            pointwise((1 - early_side, pl.ds(4 * end, 4)))
-            finish(4 * end, 4)
-            return carry
-
-        lax.fori_loop(0, 2, last, 0)
+        pointwise(patch)
+
+    for side in range(2):
+        pl.when(late[side])(functools.partial(put_columns, side))
 
     pltpu.make_async_copy(result, out, out_sem).wait()
 
-    for condition, copies in edge_sends + halo_sends:
+    for condition, copies in edge_sends + halo_sends + end_sends:
         @pl.when(condition)
         def _():
             for copy in copies:
@@ -626,20 +709,23 @@
             pltpu.VMEM((2, 49, 8, LANES), F32),
             pltpu.VMEM((FACES, 2, PADROWS * STRIDE, LANES), F32),
             pltpu.VMEM((2, ROWS, FACES, 8, CH), F32),
+            pltpu.VMEM((2, FACES, 8 * ROWS, LANES), F32),
+            pltpu.VMEM((3, FACES, ROWS, CH), F32),
             pltpu.VMEM(fields.shape, BF16),
             strip, strip,
             pltpu.VMEM((2, 2, 3, STRIP, LANES), BF16),
-            corners,
+            pltpu.VMEM((2, 2, 3, STRIP, LANES), BF16),
             pltpu.VMEM((2, 2, 3, STRIP, LANES), BF16),
             pltpu.VMEM((2, FACES, 3, COLS, CH), BF16),
             pltpu.VMEM((2, 2, 3, STRIP, LANES), BF16),
             corners,
+            pltpu.VMEM((2, 2, 3, STRIP, LANES), BF16),
             relayed,
             pltpu.VMEM((2, SIDES * FACES, 8, LANES), F32),
             relayed, relayed_half, relayed_half,
             pltpu.SemaphoreType.DMA((12,)),
-            pltpu.SemaphoreType.DMA((56,)),
-            pltpu.SemaphoreType.DMA((12,)),
+            pltpu.SemaphoreType.DMA((54,)),
+            pltpu.SemaphoreType.DMA((14,)),
             pltpu.SemaphoreType.DMA,
         ],
         compiler_params=pltpu.CompilerParams(

time: 32.8 us -> 31.7 us (0.966); the launches traced: 32.6 us -> 31.2 us
  Pallas kernels: 30.5 us -> 29.1 us
    pallas_call x1, Pallas kernels: 30.5 us -> 29.1 us  [block(): pl.pallas_call(kernel, out_shape=jax.ShapeDtypeStruct(fields.shape, BF16)...]
where the time goes in v3:
time: 31.7 us; the launch traced here: 31.2 us
  Pallas kernels  29.1 us (92%)
  local copies, waits for them, and re-layouts  2.06 us (6%)
    pallas_call x1, Pallas kernels, block(): pl.pallas_call(kernel, out_shape=jax.ShapeDtypeStruct(fields.shape, BF16)...  29.1 us
    unnamed x1, local copies, waits for them, and re-layouts  2.06 us

profile of v3, /device:TPU:0, one launch (start us, length us, event | category | flops | bytes accessed | tf_op | source)
XLA Modules:
  0.0 31.2 jit_solution(5458449544588123817)
XLA Ops:
  0.0 29.1 %convnext_block.1 = bf16[12,8,16,256]{3,2,1,0:T(8,128)(2,1)} custom-call(bf16[12,8,16,256]{3,2,1,0:T(8,128)(2,1)} %fields.1, s32[4,12]{1,0:T(4,128)} %bitcast.9, s32[4,12]{1,0:T(4,128)} %bitcast.10, f32[7,7,256]{2,1,0:T(8,128)} %conv_weight.1, f32[1,256]{1,0:T(1,128)} %bitcast.11, f32[1,256]{1,0:T(1,128)} %bitcast.12, f32[1,256]{1,0:T(1,128)} %bitcast.13, ...), custom_call_target="tpu_custom_call" | custom-call | tf_op jit(solution)/shard_map/convnext_block/pallas_call | solution.py:691
  29.1 2.1 %copy.14 = bf16[12,8,16,256]{3,2,1,0:T(8,128)(2,1)} copy(bf16[12,8,16,256]{3,2,1,0:T(8,128)(2,1)} %convnext_block.1) | data formatting | bytes 1572864

commit v4 on v3

--- a/solution.py
+++ b/solution.py
@@ -45,15 +45,15 @@
 
 
 def each_quad(body):
-    lax.fori_loop(0, FACES // 4, lambda quad, c: (body(quad), c)[1], 0)
+    lax.fori_loop(0, FACES // 4, lambda quad, c: (body(quad), c)[1], 0, unroll=3)
 
 
 def each_pair(body):
-    lax.fori_loop(0, FACES // 2, lambda pair, c: (body(pair), c)[1], 0)
+    lax.fori_loop(0, FACES // 2, lambda pair, c: (body(pair), c)[1], 0, unroll=3)
 
 
 def each_face(body):
-    lax.fori_loop(0, FACES, lambda face, c: (body(face), c)[1], 0)
+    lax.fori_loop(0, FACES, lambda face, c: (body(face), c)[1], 0, unroll=3)
 
 
 def lanes(half):

time: 31.7 us -> 30.8 us (0.972); the launches traced: 31.2 us -> 30.6 us
  Pallas kernels: 29.1 us -> 28.6 us
    pallas_call x1, Pallas kernels: 29.1 us -> 28.6 us  [block(): pl.pallas_call(kernel, out_shape=jax.ShapeDtypeStruct(fields.shape, BF16)...]
where the time goes in v4:
time: 30.8 us; the launch traced here: 30.6 us
  Pallas kernels  28.6 us (93%)
  local copies, waits for them, and re-layouts  2.06 us (7%)
    pallas_call x1, Pallas kernels, block(): pl.pallas_call(kernel, out_shape=jax.ShapeDtypeStruct(fields.shape, BF16)...  28.6 us
    unnamed x1, local copies, waits for them, and re-layouts  2.06 us

profile of v4, /device:TPU:0, one launch (start us, length us, event | category | flops | bytes accessed | tf_op | source)
XLA Modules:
  0.0 30.6 jit_solution(3109025959097561969)
XLA Ops:
  0.0 28.6 %convnext_block.1 = bf16[12,8,16,256]{3,2,1,0:T(8,128)(2,1)} custom-call(bf16[12,8,16,256]{3,2,1,0:T(8,128)(2,1)} %fields.1, s32[4,12]{1,0:T(4,128)} %bitcast.9, s32[4,12]{1,0:T(4,128)} %bitcast.10, f32[7,7,256]{2,1,0:T(8,128)} %conv_weight.1, f32[1,256]{1,0:T(1,128)} %bitcast.11, f32[1,256]{1,0:T(1,128)} %bitcast.12, f32[1,256]{1,0:T(1,128)} %bitcast.13, ...), custom_call_target="tpu_custom_call" | custom-call | tf_op jit(solution)/shard_map/convnext_block/pallas_call | solution.py:691
  28.6 2.1 %copy.14 = bf16[12,8,16,256]{3,2,1,0:T(8,128)(2,1)} copy(bf16[12,8,16,256]{3,2,1,0:T(8,128)(2,1)} %convnext_block.1) | data formatting | bytes 1572864

commit v5 on v4

--- a/solution.py
+++ b/solution.py
@@ -303,7 +303,8 @@
         pltpu.make_async_copy(buffer, buffer, recv_sems.at[recv]).wait()
 
     start_all(edge_sends)
-    start_all(halo_sends)
+    start_all(halo_sends[2:])
+    start_all(halo_sends[:2])
 
     locals_[3].wait()
     locals_[4].wait()
@@ -591,10 +592,12 @@
             def _():
                 take_seam(an_end)
                 for side in range(2):
+                    add_end(an_end, side, near[side])
+                for side in range(2):
                     pl.when((has_left, has_right)[side])(
                         functools.partial(take_corner, an_end, side, False)
                     )
-                    add_end(an_end, side, range(7))
+                    add_end(an_end, side, far[side])
 
             @pl.when(end == an_end)
             def _():
@@ -707,9 +710,9 @@
             pltpu.VMEM((1, CH), F32),
             pltpu.VMEM((1, CH), F32),
             pltpu.VMEM((2, 49, 8, LANES), F32),
-            pltpu.VMEM((FACES, 2, PADROWS * STRIDE, LANES), F32),
+            pltpu.VMEM((FACES, 2, (PADROWS + 2) * STRIDE, LANES), F32),
             pltpu.VMEM((2, ROWS, FACES, 8, CH), F32),
-            pltpu.VMEM((2, FACES, 8 * ROWS, LANES), F32),
+            pltpu.VMEM((2, FACES, 8 * ROWS + 8, LANES), F32),
             pltpu.VMEM((3, FACES, ROWS, CH), F32),
             pltpu.VMEM(fields.shape, BF16),
             strip, strip,

time: 30.8 us -> 30.7 us (level)
  no operation moved by 1% of the time
where the time goes in v5:
time: 30.7 us; the launch traced here: 30.5 us
  Pallas kernels  28.4 us (93%)
  local copies, waits for them, and re-layouts  2.06 us (7%)
    pallas_call x1, Pallas kernels, block(): pl.pallas_call(kernel, out_shape=jax.ShapeDtypeStruct(fields.shape, BF16)...  28.4 us
    unnamed x1, local copies, waits for them, and re-layouts  2.06 us

profile of v5, /device:TPU:0, one launch (start us, length us, event | category | flops | bytes accessed | tf_op | source)
XLA Modules:
  0.0 30.5 jit_solution(14544203215748643565)
XLA Ops:
  0.0 28.4 %convnext_block.1 = bf16[12,8,16,256]{3,2,1,0:T(8,128)(2,1)} custom-call(bf16[12,8,16,256]{3,2,1,0:T(8,128)(2,1)} %fields.1, s32[4,12]{1,0:T(4,128)} %bitcast.9, s32[4,12]{1,0:T(4,128)} %bitcast.10, f32[7,7,256]{2,1,0:T(8,128)} %conv_weight.1, f32[1,256]{1,0:T(1,128)} %bitcast.11, f32[1,256]{1,0:T(1,128)} %bitcast.12, f32[1,256]{1,0:T(1,128)} %bitcast.13, ...), custom_call_target="tpu_custom_call" | custom-call | tf_op jit(solution)/shard_map/convnext_block/pallas_call | solution.py:694
  28.4 2.1 %copy.14 = bf16[12,8,16,256]{3,2,1,0:T(8,128)(2,1)} copy(bf16[12,8,16,256]{3,2,1,0:T(8,128)(2,1)} %convnext_block.1) | data formatting | bytes 1572864
